TPU v7x, 128 devices: a whole 4x4x4 slice. The times are simulated.
128 devices in a mesh: row: 8 (over x, y_hi), col: 16 (over z, y_lo, core).
Axes of the slice: x: 4, y: 4 (y_hi: 2, y_lo: 2; y = y_hi * 2 + y_lo), z: 4, core: 2. Of those that a mesh axis runs over, the one named last changes fastest.
Arguments:
- currents: float32 [2, 64, 65536], P(None, None, ('row', 'col')), may hold values from -6 to 6
- projection: bfloat16 [64, 64, 65536], P(None, None, ('row', 'col')), may hold values from -0.75 to 0.75
- near_blocks: bfloat16 [4, 64, 64, 65536], P(None, None, None, ('row', 'col')), may hold values from -0.375 to 0.375
- partners: int32 [4, 65536], P(None, ('row', 'col')), may hold values from 0 to 8, as said below
- shifts: int32 [2, 65536], P(None, ('row', 'col')), may hold values from -2 to 2, as said below
- green: float32 [4096, 4096], P(('row', 'col')), may hold values from 0.5 to 2.5, as said below
Outputs:
- product: float32 [2, 64, 65536], P(None, None, ('row', 'col'))
Inputs may be any that keep to these rules, and one draw needn't show every extreme that they name: shifts[0, n] is 0 or more for elements of the first element row and 0 or less for those of the last; shifts[1, n] likewise for the first and last element columns, so that every stencil lies inside the grid. partners[0, n] is 4, the element itself; for k of 1 or more the codes of one element are distinct, each 3 (dr + 1) + (dc + 1) for offsets dr, dc in -1, 0, 1, not both 0, of an element that lies inside the array. green is the spectrum of a real even kernel: green[ky, kx] = green[(4096 - ky) % 4096, kx] = green[ky, (4096 - kx) % 4096].
All inputs are finite; a program needn't handle non-finite values.
Results may differ from a plain program's by a relative error of at most 0.0038.
Values may be sent and summed in bfloat16 or wider, within the bound.
A program may use at most 192 MiB of HBM per device.

v0:
```python
import functools
import math

import jax
import jax.numpy as jnp
import ml_dtypes
import numpy as np
from jax import lax
from jax.experimental import pallas as pl
from jax.experimental.pallas import tpu as pltpu
from jax.sharding import PartitionSpec as P

MESH = pl.DeviceIdType.MESH
F32 = jnp.float32
BF16 = jnp.bfloat16
BASIS = 64
ER = 32
EC = 16
NEIGH = 4
RHS = 2
OFFSETS = (-2, -1, 1, 2)
EDGE_SLOT = {0: 8, 1: 9, 6: 10, 7: 11}


def halves(table):
    high = np.asarray(table, np.float64).astype(ml_dtypes.bfloat16)
    low = (table - high.astype(np.float64)).astype(ml_dtypes.bfloat16)
    return np.stack([high, low])


def make_tables():
    turn = lambda rows, cols, modulus: (
        2.0 * np.pi * ((np.arange(rows)[:, None] * np.arange(cols)[None, :]) % modulus) / modulus
    )
    place = np.zeros((12, 8, 16, 256))
    for ec in range(16):
        for j in range(8):
            place[j, :, ec, 8 * ec + j] = 1
        for j in (0, 1):
            if ec < 15:
                place[EDGE_SLOT[j], :, ec, 8 * (ec + 1) + j] = 1
            else:
                place[EDGE_SLOT[j], :, ec, 128 + j] = 1
                place[EDGE_SLOT[j], :, ec, 128 + 2 + j] = 1
        for j in (6, 7):
            if ec > 0:
                place[EDGE_SLOT[j], :, ec, 8 * (ec - 1) + j] = 1
            else:
                place[EDGE_SLOT[j], :, ec, 128 + 120 + j] = 1
                place[EDGE_SLOT[j], :, ec, 128 + 118 + j] = 1
    place = place.reshape(1536, 256)
    pick = np.stack([place.T, place.T])
    real_lanes = [128 + 0, 128 + 1, 128 + 126, 128 + 127]
    imag_lanes = [128 + 2, 128 + 3, 128 + 124, 128 + 125]
    pick[0, imag_lanes] = 0
    pick[1, real_lanes] = 0
    a = turn(128, 128, 128)
    row_fwd = np.block([[np.cos(a), np.sin(a)], [-np.sin(a), np.cos(a)]])
    row_inv = np.block([[np.cos(a), np.sin(a)], [-np.sin(a), np.cos(a)]])
    b = turn(256, 128, 256)
    col_fwd = np.block([[np.cos(b), np.sin(b)], [-np.sin(b), np.cos(b)]])
    col_inv = col_fwd.T
    c = turn(16, 16, 16)
    eye = np.eye(8)
    kc, ks = np.kron(eye, np.cos(c)), np.kron(eye, np.sin(c))
    small_fwd = np.block([[kc, -ks], [ks, kc]])
    small_inv = small_fwd.T
    t1 = turn(32, 128, 4096)
    twist_row = np.stack([np.cos(t1), np.sin(t1)])
    t2 = np.tile(turn(256, 16, 4096), (1, 8))
    twist_col = np.stack([np.cos(t2), np.sin(t2)])
    half = ml_dtypes.bfloat16
    return (
        place.astype(half),
        pick.astype(half),
        halves(row_fwd),
        halves(row_inv),
        halves(col_fwd),
        halves(col_inv),
        halves(small_fwd),
        halves(small_inv),
        twist_row.astype(np.float32),
        twist_col.astype(np.float32),
    )


def dot(a, b, dims=((1,), (0,))):
    return lax.dot_general(a, b, (dims, ((), ())), preferred_element_type=F32)


def split(x):
    high = x.astype(BF16)
    return high, (x - high.astype(F32)).astype(BF16)


def cadd(a, b):
    return (a[0] + b[0], a[1] + b[1])


def csub(a, b):
    return (a[0] - b[0], a[1] - b[1])


def cmulc(a, angle):
    turns = angle / (2 * math.pi)
    quarter = round(turns * 4)
    if abs(turns * 4 - quarter) < 1e-9:
        quarter %= 4
        if quarter == 0:
            return a
        if quarter == 1:
            return (-a[1], a[0])
        if quarter == 2:
            return (-a[0], -a[1])
        return (a[1], -a[0])
    c, s = math.cos(angle), math.sin(angle)
    return (a[0] * c - a[1] * s, a[0] * s + a[1] * c)


def fft(items, sign):
    n = len(items)
    if n == 1:
        return items
    even = fft(items[0::2], sign)
    odd = fft(items[1::2], sign)
    out = [None] * n
    for k in range(n // 2):
        t = cmulc(odd[k], sign * 2 * math.pi * k / n)
        out[k] = cadd(even[k], t)
        out[k + n // 2] = csub(even[k], t)
    return out


def iota(shape, dim):
    return lax.broadcasted_iota(jnp.int32, shape, dim)


def stencil_stage(proj, curf, shifts, rows_ref):
    sub = iota((8, 128), 0)
    for g in range(4):
        lanes = slice(g * 128, (g + 1) * 128)
        dr = jnp.broadcast_to(shifts[0:1, lanes], (8, 128))
        home = (sub - dr >= 0) & (sub - dr < 8)
        cur = [curf[q, :, lanes] for q in range(RHS)]

        def body(j, carry):
            tiles = [jnp.zeros((8, 128), F32) for _ in range(RHS)]
            for i in range(8):
                weight = proj[i * 8 + j, :, lanes].astype(F32)
                for q in range(RHS):
                    line = jnp.sum(weight * cur[q], axis=0, keepdims=True)
                    tiles[q] = jnp.where(sub == i, jnp.broadcast_to(line, (8, 128)), tiles[q])
            for q in range(RHS):
                moved = tiles[q]
                for o in OFFSETS:
                    moved = jnp.where(dr == o, pltpu.roll(tiles[q], o % 8, 0), moved)
                rows_ref[q, 0, j, :, lanes] = jnp.where(home, moved, 0.0)
                rows_ref[q, 1, j, :, lanes] = jnp.where(home, 0.0, moved)
            return carry

        lax.fori_loop(0, 8, body, 0)


def spread_stage(rows_ref, shifts, place, left_ref, grid_ref, send_ref):
    sub = iota((64, 128), 0)
    lane = iota((64, 128), 1)
    own = (sub // 8) == (lane // 16)
    for g in range(4):
        lanes = slice(g * 128, (g + 1) * 128)
        dc = jnp.broadcast_to(shifts[1:2, lanes], (8, 128))
        is_offset = {o: dc == o for o in OFFSETS}

        def body(idx, carry):
            q, kind = idx // 2, lax.rem(idx, 2)
            tiles = [rows_ref[q, kind, j, :, lanes] for j in range(8)]
            for j in range(8):
                moved = tiles[j]
                for o in OFFSETS:
                    moved = jnp.where(is_offset[o], tiles[(j - o) % 8], moved)
                home = (j - dc >= 0) & (j - dc < 8)
                pieces = [(j, jnp.where(home, moved, 0.0))]
                if j in EDGE_SLOT:
                    pieces.append((EDGE_SLOT[j], jnp.where(home, 0.0, moved)))
                for slot, piece in pieces:
                    wide = jnp.where(own, jnp.concatenate([piece] * 8, axis=0), 0.0)
                    left_ref[pl.ds(pl.multiple_of(idx * 64, 64), 64), slot * 128 : (slot + 1) * 128] = (
                        wide.astype(BF16)
                    )
            return carry

        lax.fori_loop(0, 4, body, 0)
        product = dot(left_ref[...], place[...])
        for q in range(RHS):
            for kind in range(2):
                base = (q * 2 + kind) * 64
                grid_ref[q, kind, 8 + g * 64 : 8 + (g + 1) * 64, :] = product[base : base + 64]
    zero8 = jnp.zeros((8, 256), F32)
    for q in range(RHS):
        grid_ref[q, 1, 0:8, :] = zero8
        grid_ref[q, 1, 264:272, :] = zero8
    sub = lax.rem(iota((16, 256), 0), 8)
    lane1 = iota((16, 128), 1)
    real_rim = (lane1 < 2) | (lane1 >= 126)
    imag_rim = ((lane1 >= 2) & (lane1 < 4)) | ((lane1 >= 124) & (lane1 < 126))

    def message(parts):
        rim = jnp.where(real_rim, parts[0][:, 128:], jnp.where(imag_rim, parts[1][:, 128:], 0.0))
        return jnp.concatenate([parts[0][:, :128], parts[1][:, :128], rim], axis=0).astype(BF16)

    def slab(k, carry):
        parts = []
        for q in range(RHS):
            at = lambda shift: pl.ds(pl.multiple_of(k * 16 + shift, 8), 16)
            total = grid_ref[q, 0, at(8), :]
            total = total + jnp.where(sub >= 6, grid_ref[q, 1, at(16), :], 0.0)
            total = total + jnp.where(sub < 2, grid_ref[q, 1, at(0), :], 0.0)
            parts.append(total)
        send_ref[k] = message(parts)
        return carry

    lax.fori_loop(0, 16, slab, 0)
    full = iota((16, 256), 0)
    send_ref[16] = message(
        [jnp.where(full >= 14, grid_ref[q, 1, 0:16, :], 0.0) for q in range(RHS)]
    )
    send_ref[17] = message(
        [jnp.where(full < 2, grid_ref[q, 1, 256:272, :], 0.0) for q in range(RHS)]
    )


def row_forward_stage(recv, halo, has_halo, slab_ref, twist, table, mix_ref, flat_ref, out_ref):
    def widen(c, carry):
        slab_ref[c] = recv[c].astype(F32)
        return carry

    lax.fori_loop(0, 16, widen, 0)

    @pl.when(has_halo)
    def _():
        def add(c, carry):
            slab_ref[c] = slab_ref[c] + halo[c].astype(F32)
            return carry

        lax.fori_loop(0, 16, add, 0)

    lane = iota((8, 128), 1)

    def rows(h, carry):
        at = lambda start: pl.ds(pl.multiple_of(start + h * 8, 8), 8)
        rims = [slab_ref[c, at(32), :] for c in range(16)]
        items = []
        for c in range(16):
            real = slab_ref[c, at(0), :]
            imag = slab_ref[c, at(16), :]
            if c > 0:
                real = real + jnp.where(lane < 2, rims[c - 1], 0.0)
                imag = imag + jnp.where(lane < 2, pltpu.roll(rims[c - 1], 126, 1), 0.0)
            if c < 15:
                real = real + jnp.where(lane >= 126, rims[c + 1], 0.0)
                imag = imag + jnp.where(lane >= 126, pltpu.roll(rims[c + 1], 2, 1), 0.0)
            items.append((real, imag))
        even = fft(items, -1)
        odd = fft([cmulc(v, -2 * math.pi * c / 32) for c, v in enumerate(items)], -1)
        for m in range(16):
            for p, (real, imag) in enumerate((even[m], odd[m])):
                k0 = 2 * m + p
                cos, sin = twist[0, k0 : k0 + 1, :], twist[1, k0 : k0 + 1, :]
                mix_ref[at(k0 * 16), 0:128] = real * cos + imag * sin
                mix_ref[at(k0 * 16), 128:256] = imag * cos - real * sin
        return carry

    lax.fori_loop(0, 2, rows, 0)
    high, low = split(mix_ref[...])
    nt = ((1,), (1,))
    out = dot(table[0], high, nt) + dot(table[1], high, nt) + dot(table[0], low, nt)
    to_messages(out, flat_ref, out_ref)


def to_messages(out, flat_ref, out_ref):
    for ri in range(2):
        for g in range(4):
            flat_ref[pl.ds(ri * 4 + g, 128, stride=8), :] = out[
                ri * 128 : (ri + 1) * 128, g * 128 : (g + 1) * 128
            ]
    out_ref[...] = flat_ref[...].reshape(128, 8, 128).astype(BF16)


def from_messages(recv, flat_ref, half_ref):
    flat_ref[...] = recv[...].astype(F32).reshape(1024, 128)
    for ri in range(2):
        for g in range(4):
            half_ref[ri * 128 : (ri + 1) * 128, g * 128 : (g + 1) * 128] = flat_ref[
                pl.ds(ri * 4 + g, 128, stride=8), :
            ].astype(BF16)


def column_stage(recv, flat_ref, half_ref, fwd, inv, small, small_inv, twist, green, wide_ref, out_ref):
    from_messages(recv, flat_ref, half_ref)
    block = half_ref[...]
    wide_ref[...] = dot(fwd[0], block) + dot(fwd[1], block)
    cos, sin = twist[0], twist[1]
    for g in range(4):
        lanes = slice(g * 128, (g + 1) * 128)
        real, imag = wide_ref[0:256, lanes], wide_ref[256:512, lanes]
        turned = jnp.concatenate([real * cos + imag * sin, imag * cos - real * sin], axis=1)
        high, low = split(turned)
        spec = dot(high, small[0]) + dot(low, small[0]) + dot(high, small[1])
        scale = green[:, lanes]
        spec = spec * jnp.concatenate([scale, scale], axis=1)
        high, low = split(spec)
        back = dot(high, small_inv[0]) + dot(low, small_inv[0]) + dot(high, small_inv[1])
        real, imag = back[:, 0:128], back[:, 128:256]
        wide_ref[0:256, lanes] = real * cos - imag * sin
        wide_ref[256:512, lanes] = imag * cos + real * sin
    high, low = split(wide_ref[...])
    out = dot(inv[0], high) + dot(inv[0], low) + dot(inv[1], high)
    to_messages(out, flat_ref, out_ref)


def row_inverse_stage(recv, flat_ref, half_ref, table, twist, mix_ref, slab_ref, send_ref):
    from_messages(recv, flat_ref, half_ref)
    turned = half_ref[...].T
    mix_ref[...] = dot(turned, table[0]) + dot(turned, table[1])

    def rows(h, carry):
        at = lambda start: pl.ds(pl.multiple_of(start + h * 8, 8), 8)
        items = []
        for k0 in range(32):
            cos, sin = twist[0, k0 : k0 + 1, :], twist[1, k0 : k0 + 1, :]
            real, imag = mix_ref[at(k0 * 16), 0:128], mix_ref[at(k0 * 16), 128:256]
            items.append((real * cos - imag * sin, imag * cos + real * sin))
        even = fft(items[0::2], 1)
        odd = fft(items[1::2], 1)
        for c in range(16):
            real, imag = cadd(even[c], cmulc(odd[c], 2 * math.pi * c / 32))
            slab_ref[c, at(0), :] = real
            slab_ref[c, at(16), :] = imag
        return carry

    lax.fori_loop(0, 2, rows, 0)
    lane = iota((16, 128), 1)
    for c in range(16):
        rim = jnp.zeros((16, 128), F32)
        if c < 15:
            rim = jnp.where(lane < 2, slab_ref[c + 1, 0:16, :], rim)
            rim = jnp.where((lane >= 2) & (lane < 4), pltpu.roll(slab_ref[c + 1, 16:32, :], 2, 1), rim)
        if c > 0:
            rim = jnp.where(lane >= 126, slab_ref[c - 1, 0:16, :], rim)
            rim = jnp.where(
                (lane >= 124) & (lane < 126), pltpu.roll(slab_ref[c - 1, 16:32, :], 126, 1), rim
            )
        send_ref[c] = jnp.concatenate([slab_ref[c, 0:32, :], rim], axis=0).astype(BF16)


def sample_stage(recv, pick, shifts, tall_ref, rows_ref, sample_ref):
    sub = iota((8, 128), 0)
    lane = iota((8, 128), 1)
    owns = [(lane // 16) == e for e in range(8)]
    for q in range(RHS):
        main = recv[:, q * 16 : (q + 1) * 16, :].reshape(288, 128)
        rim = recv[:, 32:48, :].reshape(288, 128)
        tall_ref[...] = dot(jnp.concatenate([main, rim], axis=1), pick[q])
        for g in range(4):
            lanes = slice(g * 128, (g + 1) * 128)
            dr = jnp.broadcast_to(shifts[0:1, lanes], (8, 128))
            dc = jnp.broadcast_to(shifts[1:2, lanes], (8, 128))

            def body(slot, carry):
                column = pl.ds(pl.multiple_of(slot * 128, 128), 128)
                tiles = [
                    tall_ref[8 + 64 * g + 8 * t : 16 + 64 * g + 8 * t, column] for t in range(10)
                ]
                home = tiles[1]
                edge = jnp.where(sub < 4, tiles[2], tiles[0])
                for e in range(1, 8):
                    home = jnp.where(owns[e], tiles[e + 1], home)
                    edge = jnp.where(owns[e], jnp.where(sub < 4, tiles[e + 2], tiles[e]), edge)
                moved = home
                for o in OFFSETS:
                    kept = (sub >= o) if o > 0 else (sub < 8 + o)
                    shifted = pltpu.roll(jnp.where(kept, home, edge), (-o) % 8, 0)
                    moved = jnp.where(dr == o, shifted, moved)
                rows_ref[slot] = moved
                return carry

            lax.fori_loop(0, 12, body, 0)
            line = lambda j: rows_ref[j] if 0 <= j < 8 else rows_ref[EDGE_SLOT[j % 8]]
            for j in range(8):
                moved = line(j)
                for o in OFFSETS:
                    moved = jnp.where(dc == o, line(j + o), moved)
                sample_ref[q, j, :, lanes] = moved


def far_stage(proj, sample_ref, near_ref, out_ref):
    for g in range(4):
        lanes = slice(g * 128, (g + 1) * 128)

        def body(j, sums):
            sums = list(sums)
            for i in range(8):
                weight = proj[i * 8 + j, :, lanes].astype(F32)
                for q in range(RHS):
                    line = sample_ref[q, j, i : i + 1, lanes]
                    sums[q] = sums[q] + weight * line
            return tuple(sums)

        sums = lax.fori_loop(0, 8, body, tuple(near_ref[q, :, lanes] for q in range(RHS)))
        for q in range(RHS):
            out_ref[q, :, lanes] = sums[q]


def turn_green(green, rows_ref, out_ref):
    for j1 in range(16):
        for h in range(2):
            rows_ref[h, pl.ds(j1, 32, stride=16), :] = green[
                :, j1 * 256 + h * 128 : j1 * 256 + (h + 1) * 128
            ]
    for h in range(2):
        for g in range(4):
            out_ref[h * 128 : (h + 1) * 128, g * 128 : (g + 1) * 128] = rows_ref[
                h, g * 128 : (g + 1) * 128, :
            ].T * (1.0 / 16777216)


def slots_wait(ref, count, sem):
    part = ref.at[pl.ds(0, count)]
    pltpu.make_async_copy(part, part, sem).wait()


def main_kernel(
    cur, proj, shifts, green, near,
    place, pick, row_fwd, row_inv, col_fwd, col_inv, small, small_inv, twist_row, twist_col,
    out_ref,
    rows_ref, left_ref, grid_ref, send1, recv1, halo1, slab_ref, mix_ref, flat_ref, send2, recv2,
    half_ref, wide_ref, green_rows, green_turned, send3, recv3, send4, recv4, tall_ref, pick_rows,
    sample_ref, curf,
    ssem, rsem, hsem, lsem,
):
    r, c = lax.axis_index("row"), lax.axis_index("col")
    me = r * 16 + c
    barrier = pltpu.get_barrier_semaphore()

    def peer(k):
        d = lax.rem(me + k, 128)
        return d, (d // 16, lax.rem(d, 16))

    def greet(k, carry):
        pl.semaphore_signal(barrier, inc=1, device_id=peer(k)[1], device_id_type=MESH)
        return carry

    zero = jnp.zeros((48, 128), BF16)
    recv4[0] = zero
    recv4[17] = zero
    lax.fori_loop(1, 128, greet, 0)
    curf[...] = cur[...].astype(BF16).astype(F32)
    stencil_stage(proj, curf, shifts, rows_ref)
    spread_stage(rows_ref, shifts, place, left_ref, grid_ref, send1)
    pl.semaphore_wait(barrier, 127)

    def to_column(send, recv, slot, index):
        def go(k, carry):
            d = lax.rem(c + k, 16)
            pltpu.make_async_remote_copy(
                send.at[d], recv.at[slot], ssem.at[index], rsem.at[index], device_id=(r, d), device_id_type=MESH
            ).start()
            return carry

        lax.fori_loop(1, 16, go, 0)

    to_column(send1, recv1, c, 0)

    @pl.when(r > 0)
    def _():
        pltpu.make_async_remote_copy(
            send1.at[16], halo1.at[c], ssem.at[4], hsem.at[0], device_id=(r - 1, 15), device_id_type=MESH
        ).start()

    @pl.when(r < 7)
    def _():
        pltpu.make_async_remote_copy(
            send1.at[17], halo1.at[c], ssem.at[5], hsem.at[0], device_id=(r + 1, 0), device_id_type=MESH
        ).start()

    own = pltpu.make_async_copy(send1.at[c], recv1.at[c], lsem.at[0])
    own.start()
    turn_green(green, green_rows, green_turned)
    own.wait()
    has_halo = ((c == 0) & (r > 0)) | ((c == 15) & (r < 7))
    slots_wait(recv1, 15, rsem.at[0])

    @pl.when(has_halo)
    def _():
        slots_wait(halo1, 16, hsem.at[0])

    row_forward_stage(recv1, halo1, has_halo, slab_ref, twist_row, row_fwd, mix_ref, flat_ref, send2)

    def to_all(send, recv, index):
        def go(k, carry):
            d, where = peer(k)
            pltpu.make_async_remote_copy(
                send.at[d], recv.at[me], ssem.at[index], rsem.at[index], device_id=where, device_id_type=MESH
            ).start()
            return carry

        own = pltpu.make_async_copy(send.at[me], recv.at[me], lsem.at[index])
        own.start()
        lax.fori_loop(1, 128, go, 0)
        own.wait()
        slots_wait(recv, 127, rsem.at[index])

    to_all(send2, recv2, 1)
    column_stage(
        recv2, flat_ref, half_ref, col_fwd, col_inv, small, small_inv, twist_col, green_turned, wide_ref, send3
    )
    to_all(send3, recv3, 2)
    row_inverse_stage(recv3, flat_ref, half_ref, row_inv, twist_row, mix_ref, slab_ref, send4)
    to_column(send4, recv4, c + 1, 3)

    def to_neighbour_row(target, slot, index, sem):
        def go(d, carry):
            pltpu.make_async_remote_copy(
                send4.at[d], recv4.at[slot], ssem.at[index], hsem.at[sem], device_id=(target, d), device_id_type=MESH
            ).start()
            return carry

        lax.fori_loop(0, 16, go, 0)

    up = (c == 0) & (r > 0)
    down = (c == 15) & (r < 7)

    @pl.when(up)
    def _():
        to_neighbour_row(r - 1, 17, 6, 1)

    @pl.when(down)
    def _():
        to_neighbour_row(r + 1, 0, 7, 2)

    own = pltpu.make_async_copy(send4.at[c], recv4.at[c + 1], lsem.at[3])
    own.start()
    own.wait()
    slots_wait(recv4, 15, rsem.at[3])

    @pl.when(r < 7)
    def _():
        slots_wait(recv4, 1, hsem.at[1])

    @pl.when(r > 0)
    def _():
        slots_wait(recv4, 1, hsem.at[2])

    sample_stage(recv4, pick, shifts, tall_ref, pick_rows, sample_ref)
    far_stage(proj, sample_ref, near, out_ref)

    slots_wait(send1, 15, ssem.at[0])

    @pl.when(r > 0)
    def _():
        slots_wait(send1, 1, ssem.at[4])

    @pl.when(r < 7)
    def _():
        slots_wait(send1, 1, ssem.at[5])

    slots_wait(send2, 127, ssem.at[1])
    slots_wait(send3, 127, ssem.at[2])
    slots_wait(send4, 15, ssem.at[3])

    @pl.when(up)
    def _():
        slots_wait(send4, 16, ssem.at[6])

    @pl.when(down)
    def _():
        slots_wait(send4, 16, ssem.at[7])


def main_call(cur, proj, shifts, green, near):
    tables = [jnp.asarray(t) for t in make_tables()]
    vmem = pl.BlockSpec(memory_space=pltpu.VMEM)
    dma = pltpu.SemaphoreType.DMA
    return pl.pallas_call(
        main_kernel,
        out_shape=jax.ShapeDtypeStruct((RHS, BASIS, ER * EC), F32),
        in_specs=[vmem] * (5 + len(tables)),
        out_specs=vmem,
        scratch_shapes=[
            pltpu.VMEM((RHS, 2, 8, 8, 512), F32),
            pltpu.VMEM((256, 1536), BF16),
            pltpu.VMEM((RHS, 2, 272, 256), F32),
            pltpu.VMEM((18, 48, 128), BF16),
            pltpu.VMEM((16, 48, 128), BF16),
            pltpu.VMEM((16, 48, 128), BF16),
            pltpu.VMEM((16, 48, 128), F32),
            pltpu.VMEM((512, 256), F32),
            pltpu.VMEM((1024, 128), F32),
            pltpu.VMEM((128, 8, 128), BF16),
            pltpu.VMEM((128, 8, 128), BF16),
            pltpu.VMEM((256, 512), BF16),
            pltpu.VMEM((512, 512), F32),
            pltpu.VMEM((2, 512, 128), F32),
            pltpu.VMEM((256, 512), F32),
            pltpu.VMEM((128, 8, 128), BF16),
            pltpu.VMEM((128, 8, 128), BF16),
            pltpu.VMEM((16, 48, 128), BF16),
            pltpu.VMEM((18, 48, 128), BF16),
            pltpu.VMEM((288, 1536), F32),
            pltpu.VMEM((12, 8, 128), F32),
            pltpu.VMEM((RHS, 8, 8, 512), F32),
            pltpu.VMEM((RHS, BASIS, 512), F32),
            dma((8,)),
            dma((4,)),
            dma((3,)),
            dma((4,)),
        ],
        compiler_params=pltpu.CompilerParams(
            collective_id=0, has_side_effects=True, vmem_limit_bytes=48 * 2**20
        ),
    )(cur, proj, shifts, green, near, *tables)


def near_kernel(blocks, picked, out_ref):
    for g in range(4):
        lanes = slice(g * 128, (g + 1) * 128)

        def body(step, sums):
            k, b = step // 4, lax.rem(step, 4)
            at = pl.ds(pl.multiple_of(b * 16, 16), 16)
            values = [picked[k, q, at, lanes].astype(F32) for q in range(RHS)]
            sums = list(sums)
            for a in range(8):
                weight = blocks[k, a, at, lanes].astype(F32)
                for q in range(RHS):
                    product = weight * values[q]
                    sums[a * 2 + q] = sums[a * 2 + q] + (product[0:8] + product[8:16])
            return tuple(sums)

        sums = lax.fori_loop(0, 16, body, tuple(jnp.zeros((8, 128), F32) for _ in range(16)))
        sub = iota((8, 128), 0)
        for q in range(RHS):
            tile = jnp.zeros((8, 128), F32)
            for a in range(8):
                line = jnp.sum(sums[a * 2 + q], axis=0, keepdims=True)
                tile = jnp.where(sub == a, jnp.broadcast_to(line, (8, 128)), tile)
            out_ref[q, :, lanes] = tile


def near_call(blocks, picked):
    return pl.pallas_call(
        near_kernel,
        grid=(8,),
        out_shape=jax.ShapeDtypeStruct((RHS, BASIS, ER * EC), F32),
        in_specs=[
            pl.BlockSpec((NEIGH, 8, BASIS, ER * EC), lambda a: (0, a, 0, 0)),
            pl.BlockSpec((NEIGH, RHS, BASIS, ER * EC), lambda a: (0, 0, 0, 0)),
        ],
        out_specs=pl.BlockSpec((RHS, 8, ER * EC), lambda a: (0, a, 0)),
        compiler_params=pltpu.CompilerParams(vmem_limit_bytes=24 * 2**20),
    )(blocks, picked)


def extended_2(block, sides, width):
    for axis, dim in sides:
        count = lax.axis_size(axis)
        forward = [(i, i + 1) for i in range(count - 1)]
        backward = [(target, source) for source, target in forward]
        low = lax.ppermute(
            lax.slice_in_dim(block, block.shape[dim] - width, None, axis=dim), axis, forward
        )
        high = lax.ppermute(lax.slice_in_dim(block, 0, width, axis=dim), axis, backward)
        block = jnp.concatenate([low, block, high], axis=dim)
    return block


def shards(currents, projection, near_blocks, partners, shifts, green):
    elements = ER * EC
    cur_half = currents.astype(BF16)
    spread = extended_2(cur_half.reshape(RHS, BASIS, ER, EC), (("row", 2), ("col", 3)), 1)
    views = []
    for symbol in range(9):
        row_start, col_start = symbol // 3, symbol % 3
        views.append(
            spread[:, :, row_start : row_start + ER, col_start : col_start + EC].reshape(
                RHS, BASIS, elements
            )
        )
    picked = []
    for slot in range(NEIGH):
        chosen = jnp.zeros((RHS, BASIS, elements), BF16)
        for symbol in range(9):
            chosen = jnp.where(partners[slot] == symbol, views[symbol], chosen)
        picked.append(chosen)
    near = near_call(near_blocks, jnp.stack(picked))
    return main_call(currents, projection, shifts, green, near)


def solution(mesh):
    in_specs = (
        P(None, None, ("row", "col")),
        P(None, None, ("row", "col")),
        P(None, None, None, ("row", "col")),
        P(None, ("row", "col")),
        P(None, ("row", "col")),
        P(("row", "col"), None),
    )
    out_specs = P(None, None, ("row", "col"))
    return jax.shard_map(shards, mesh=mesh, in_specs=in_specs, out_specs=out_specs, check_vma=False)
```

profile of v0, /device:TPU:1, one launch (start us, length us, event | category | flops | bytes accessed | tf_op | source)
XLA Modules:
  0.0 94.2 jit_solution(4715556591648205319)
XLA Ops:
  0.0 1.0 %convert_element_type.3 = bf16[2,64,512]{2,1,0:T(8,128)(2,1)S(1)} convert(f32[2,64,512]{2,1,0:T(8,128)} %cur.1) | non-fusion elementwise | flops 65536 | bytes 393216 | tf_op jit(solution)/shard_map/convert_element_type | solution.py:678
  1.0 0.2 copy.17
  1.2 5.6 %collective-permute-start = (bf16[2,64,1,16]{1,3,2,0:T(8,128)(2,1)S(1)}, bf16[2,64,1,16]{1,3,2,0:T(8,128)(2,1)S(1)}, u32[]{:S(2)}, u32[]{:S(2)}) collective-permute-start(bf16[2,64,1,16]{1,3,2,0:T(8,128)(2,1)S(1)} %get-tuple-element.53), channel_id=1, source_target_pairs={{0,16},{16,32},{32,48},{48,64},{64,80},{80,96},{96,112},{1,17},{17... | collective-permute-start | bytes 12296 | tf_op jit(solution)/shard_map/ppermute | solution.py:668
  6.8 1.3 %collective-permute-start.1 = (bf16[2,64,1,16]{1,3,2,0:T(8,128)(2,1)S(1)}, bf16[2,64,1,16]{1,3,2,0:T(8,128)(2,1)S(1)}, u32[]{:S(2)}, u32[]{:S(2)}) collective-permute-start(bf16[2,64,1,16]{1,3,2,0:T(8,128)(2,1)S(1)} %get-tuple-element.54), channel_id=1, source_target_pairs={{16,0},{32,16},{48,32},{64,48},{80,64},{96,80},{112,96},{17,1},{33... | collective-permute-start | bytes 12296 | tf_op jit(solution)/shard_map/ppermute | solution.py:671
  8.1 1.1 %compare_reduce_fusion.35 = (pred[512]{0:T(512)(128)(4,1)S(1)}, pred[512]{0:T(512)(128)(4,1)S(1)}, pred[512]{0:T(512)(128)(4,1)S(1)}, pred[512]{0:T(512)(128)(4,...) fusion(s32[4,512]{1,0:T(4,128)} %param.19), kind=kLoop, calls=%fused_computation.47 | loop fusion | flops 18432 | bytes 26624 | tf_op jit(solution)/shard_map/eq | solution.py:692
  9.2 0.0 collective-permute-done
  9.3 3.5 %collective-permute-done.1 = bf16[2,64,1,16]{1,3,2,0:T(8,128)(2,1)S(1)} collective-permute-done((bf16[2,64,1,16]{1,3,2,0:T(8,128)(2,1)S(1)}, bf16[2,64,1,16]{1,3,2,0:T(8,128)(2,1)S(1)}, u32[]{:S(2)}, u32[]{:S(2)}) %collective-permute-start.1) | collective-permute-done | bytes 4128 | tf_op jit(solution)/shard_map/ppermute | solution.py:671
  12.7 0.1 pad_maximum_fusion.4
  12.8 0.0 copy-start.1
  12.8 4.1 %collective-permute-start.2 = (bf16[2,64,34,1]{1,3,2,0:T(2,128)(2,1)S(1)}, bf16[2,64,34,1]{1,3,2,0:T(2,128)(2,1)S(1)}, u32[]{:S(2)}, u32[]{:S(2)}) collective-permute-start(bf16[2,64,34,1]{1,3,2,0:T(2,128)(2,1)S(1)} %get-tuple-element.50), channel_id=1, source_target_pairs={{1,0},{2,1},{3,2},{4,3},{5,4},{6,5},{7,6},{8,7},{9,8},{10,9},{11,1... | collective-permute-start | bytes 26120 | tf_op jit(solution)/shard_map/ppermute | solution.py:671
  17.0 2.2 %collective-permute-start.3 = (bf16[2,64,34,1]{1,3,2,0:T(2,128)(2,1)S(1)}, bf16[2,64,34,1]{1,3,2,0:T(2,128)(2,1)S(1)}, u32[]{:S(2)}, u32[]{:S(2)}) collective-permute-start(bf16[2,64,34,1]{1,3,2,0:T(2,128)(2,1)S(1)} %get-tuple-element.49), channel_id=1, source_target_pairs={{0,1},{1,2},{2,3},{3,4},{4,5},{5,6},{6,7},{7,8},{8,9},{9,10},{10,1... | collective-permute-start | bytes 26120 | tf_op jit(solution)/shard_map/ppermute | solution.py:668
  19.2 0.1 pad_maximum_fusion.2
  19.2 0.1 copy.19
  19.4 0.1 copy.24
  19.5 0.0 collective-permute-done.2
  19.5 0.7 collective-permute-done.3
  20.2 0.2 maximum_maximum_fusion
  20.4 0.2 fusion
  20.7 0.1 copy.18
  20.8 0.1 copy.20
  20.9 0.1 copy.21
  21.1 0.1 copy.22
  21.2 0.1 copy.23
  21.3 0.1 copy.25
  21.5 0.0 copy-done.1
  21.5 0.1 select_bitcast_fusion.3
  21.6 0.1 select_bitcast_fusion.2
  21.6 0.1 select_bitcast_fusion.1
  21.7 0.1 select_bitcast_fusion
  21.8 0.1 pad_maximum_fusion.picked
  21.9 0.0 copy-start
  21.9 5.8 %copy-done = bf16[4,64,64,512]{3,2,1,0:T(8,128)(2,1)S(1)} copy-done((bf16[4,64,64,512]{3,2,1,0:T(8,128)(2,1)S(1)}, bf16[4,64,64,512]{3,2,1,0:T(8,128)(2,1)}, u32[]{:S(2)}) %copy-start) | copy-done | bytes 16777240
  27.7 0.0 copy-start.6
  27.7 0.0 copy-start.7
  27.7 0.0 copy-start.8
  27.7 0.0 copy-start.9
  27.7 0.0 copy-start.10
  27.7 0.0 copy-start.11
  27.8 0.0 copy-start.12
  27.8 14.8 %shard_map.154.near = f32[2,64,512]{2,1,0:T(8,128)S(1)} custom-call(bf16[4,64,64,512]{3,2,1,0:T(8,128)(2,1)S(1)} %copy-done, bf16[4,2,64,512]{3,2,1,0:T(8,128)(2,1)S(1)} %pad_maximum_fusion.picked), custom_call_target="tpu_custom_call" | custom-call | tf_op jit(solution)/shard_map/pallas_call | solution.py:650
  42.6 0.0 copy-done.2
  42.6 0.0 copy-done.3
  42.6 0.0 copy-done.4
  42.6 0.0 copy-done.5
  42.6 0.0 copy-done.6
  42.6 0.0 copy-done.7
  42.7 50.8 %shard_map.155 = f32[2,64,512]{2,1,0:T(8,128)S(1)} custom-call(f32[2,64,512]{2,1,0:T(8,128)S(1)} %copy-done.1, bf16[64,64,512]{2,1,0:T(8,128)(2,1)} %proj.1, s32[2,512]{1,0:T(2,128)S(1)} %copy-done.12, f32[32,4096]{1,0:T(8,128)S(1)} %copy-done.5, f32[2,64,512]{2,1,0:T(8,128)S(1)} %shard_map.154.near, bf16[1536,256]{1,0:T(8,128)(2,1)S(1)} %copy-done.4, ...), custom_call_target="tpu_custom_call" | custom-call | tf_op jit(solution)/shard_map/pallas_call | solution.py:583
  93.5 0.7 copy.51
  (10 shorter events, 0.0 us)
Async XLA Ops:
  1.2 8.1 %collective-permute-start = (bf16[2,64,1,16]{1,3,2,0:T(8,128)(2,1)S(1)}, bf16[2,64,1,16]{1,3,2,0:T(8,128)(2,1)S(1)}, u32[]{:S(2)}, u32[]{:S(2)}) collective-permute-start(bf16[2,64,1,16]{1,3,2,0:T(8,128)(2,1)S(1)} %get-tuple-element.53), channel_id=1, source_target_pairs={{0,16},{16,32},{32,48},{48,64},{64,80},{80,96},{96,112},{1,17},{17... | collective-permute-start | bytes 12296 | tf_op jit(solution)/shard_map/ppermute | solution.py:668
  6.8 5.9 %collective-permute-start.1 = (bf16[2,64,1,16]{1,3,2,0:T(8,128)(2,1)S(1)}, bf16[2,64,1,16]{1,3,2,0:T(8,128)(2,1)S(1)}, u32[]{:S(2)}, u32[]{:S(2)}) collective-permute-start(bf16[2,64,1,16]{1,3,2,0:T(8,128)(2,1)S(1)} %get-tuple-element.54), channel_id=1, source_target_pairs={{16,0},{32,16},{48,32},{64,48},{80,64},{96,80},{112,96},{17,1},{33... | collective-permute-start | bytes 12296 | tf_op jit(solution)/shard_map/ppermute | solution.py:671
  12.8 8.7 %copy-start.1 = (f32[2,64,512]{2,1,0:T(8,128)S(1)}, f32[2,64,512]{2,1,0:T(8,128)}, u32[]{:S(2)}) copy-start(f32[2,64,512]{2,1,0:T(8,128)} %cur.1) | copy-start | bytes 786436
  12.8 6.7 %collective-permute-start.2 = (bf16[2,64,34,1]{1,3,2,0:T(2,128)(2,1)S(1)}, bf16[2,64,34,1]{1,3,2,0:T(2,128)(2,1)S(1)}, u32[]{:S(2)}, u32[]{:S(2)}) collective-permute-start(bf16[2,64,34,1]{1,3,2,0:T(2,128)(2,1)S(1)} %get-tuple-element.50), channel_id=1, source_target_pairs={{1,0},{2,1},{3,2},{4,3},{5,4},{6,5},{7,6},{8,7},{9,8},{10,9},{11,1... | collective-permute-start | bytes 26120 | tf_op jit(solution)/shard_map/ppermute | solution.py:671
  17.0 3.2 %collective-permute-start.3 = (bf16[2,64,34,1]{1,3,2,0:T(2,128)(2,1)S(1)}, bf16[2,64,34,1]{1,3,2,0:T(2,128)(2,1)S(1)}, u32[]{:S(2)}, u32[]{:S(2)}) collective-permute-start(bf16[2,64,34,1]{1,3,2,0:T(2,128)(2,1)S(1)} %get-tuple-element.49), channel_id=1, source_target_pairs={{0,1},{1,2},{2,3},{3,4},{4,5},{5,6},{6,7},{7,8},{8,9},{9,10},{10,1... | collective-permute-start | bytes 26120 | tf_op jit(solution)/shard_map/ppermute | solution.py:668
  21.9 5.8 %copy-start = (bf16[4,64,64,512]{3,2,1,0:T(8,128)(2,1)S(1)}, bf16[4,64,64,512]{3,2,1,0:T(8,128)(2,1)}, u32[]{:S(2)}) copy-start(bf16[4,64,64,512]{3,2,1,0:T(8,128)(2,1)} %blocks.1) | copy-start | bytes 50331652
  27.7 14.9 %copy-start.2 = (bf16[2,256,1536]{2,1,0:T(8,128)(2,1)S(1)}, bf16[2,256,1536]{2,1,0:T(8,128)(2,1)}, u32[]{:S(2)}) copy-start(bf16[2,256,1536]{2,1,0:T(8,128)(2,1)} %constant.39.clone.pick) | copy-start | bytes 4718596
  27.7 14.9 %copy-start.3 = (bf16[2,256,256]{2,1,0:T(8,128)(2,1)S(1)}, bf16[2,256,256]{2,1,0:T(8,128)(2,1)}, u32[]{:S(2)}) copy-start(bf16[2,256,256]{2,1,0:T(8,128)(2,1)} %constant.40.clone.row_fwd.row_inv) | copy-start | bytes 786436
  27.7 14.9 %copy-start.4 = (bf16[1536,256]{1,0:T(8,128)(2,1)S(1)}, bf16[1536,256]{1,0:T(8,128)(2,1)}, u32[]{:S(2)}) copy-start(bf16[1536,256]{1,0:T(8,128)(2,1)} %constant.38.clone.place) | copy-start | bytes 2359300
  27.7 14.9 %copy-start.5 = (f32[32,4096]{1,0:T(8,128)S(1)}, f32[32,4096]{1,0:T(8,128)}, u32[]{:S(2)}) copy-start(f32[32,4096]{1,0:T(8,128)} %green.1) | copy-start | bytes 1572868
  27.7 14.9 %copy-start.6 = (bf16[2,512,256]{2,1,0:T(8,128)(2,1)S(1)}, bf16[2,512,256]{2,1,0:T(8,128)(2,1)}, u32[]{:S(2)}) copy-start(bf16[2,512,256]{2,1,0:T(8,128)(2,1)} %constant.41.clone.col_fwd) | copy-start | bytes 1572868
  27.7 14.9 %copy-start.7 = (bf16[2,256,512]{2,1,0:T(8,128)(2,1)S(1)}, bf16[2,256,512]{2,1,0:T(8,128)(2,1)}, u32[]{:S(2)}) copy-start(bf16[2,256,512]{2,1,0:T(8,128)(2,1)} %constant.42.clone.col_inv) | copy-start | bytes 1572868
  27.7 14.9 %copy-start.8 = (bf16[2,256,256]{2,1,0:T(8,128)(2,1)S(1)}, bf16[2,256,256]{2,1,0:T(8,128)(2,1)}, u32[]{:S(2)}) copy-start(bf16[2,256,256]{2,1,0:T(8,128)(2,1)} %constant.43.clone.small) | copy-start | bytes 786436
  27.7 14.9 %copy-start.9 = (bf16[2,256,256]{2,1,0:T(8,128)(2,1)S(1)}, bf16[2,256,256]{2,1,0:T(8,128)(2,1)}, u32[]{:S(2)}) copy-start(bf16[2,256,256]{2,1,0:T(8,128)(2,1)} %constant.44.clone.small_inv) | copy-start | bytes 786436
  27.7 14.9 %copy-start.10 = (f32[2,256,128]{2,1,0:T(8,128)S(1)}, f32[2,256,128]{2,1,0:T(8,128)}, u32[]{:S(2)}) copy-start(f32[2,256,128]{2,1,0:T(8,128)} %constant.46.clone.twist_col) | copy-start | bytes 786436
  27.7 14.9 %copy-start.11 = (f32[2,32,128]{2,1,0:T(8,128)S(1)}, f32[2,32,128]{2,1,0:T(8,128)}, u32[]{:S(2)}) copy-start(f32[2,32,128]{2,1,0:T(8,128)} %constant.45.clone.twist_row) | copy-start | bytes 98308
  27.8 14.9 %copy-start.12 = (s32[2,512]{1,0:T(2,128)S(1)}, s32[2,512]{1,0:T(2,128)}, u32[]{:S(2)}) copy-start(s32[2,512]{1,0:T(2,128)} %shifts.1) | copy-start | bytes 12292
where the time goes:
time: 94.6 us; the launch traced here: 94.2 us
  Pallas kernels  65.6 us (69%)
  starting transfers between devices  13.3 us (14%)
  local copies, waits for them, and re-layouts  7.94 us (8%)
  waiting for transfers between devices  4.14 us (4%)
  other arithmetic  2.86 us (3%)
    pallas_call x1, Pallas kernels, main_call(): pl.pallas_call(main_kernel, out_shape=jax.ShapeDtypeStruct((RHS, BASIS, E...  50.8 us
    pallas_call x1, Pallas kernels, near_call(): pl.pallas_call(near_kernel, grid=(8,), out_shape=jax.ShapeDtypeStruct((RH...  14.8 us
    ppermute x2, starting transfers between devices, extended_2(): lax.ppermute(lax.slice_in_dim(block, block.shape[dim] - width, None, axis...  7.85 us
    unnamed x27, local copies, waits for them, and re-layouts  6.54 us
    ppermute x2, starting transfers between devices, extended_2(): lax.ppermute(lax.slice_in_dim(block, 0, width, axis=dim), axis, backward)  5.44 us
    ppermute x2, waiting for transfers between devices, extended_2(): lax.ppermute(lax.slice_in_dim(block, 0, width, axis=dim), axis, backward)  3.46 us
  transfers between devices with their start and end apart: 4, of which 2 were waited for; matrix products, arithmetic and copies ran while one was open for 2% of the time, Pallas kernels for 0%

commit v1 on v0

--- a/solution.py
+++ b/solution.py
@@ -135,7 +135,35 @@
     return lax.broadcasted_iota(jnp.int32, shape, dim)
 
 
-def stencil_stage(proj, curf, shifts, rows_ref):
+def row_sums(tiles):
+    sub = iota((8, 128), 0)
+    top = sub < 4
+    tiles = [
+        jnp.where(top, tiles[i], tiles[i + 4])
+        + pltpu.roll(jnp.where(top, tiles[i + 4], tiles[i]), 4, 0)
+        for i in range(4)
+    ]
+    for step in (2, 1):
+        upper = lax.rem(sub, 2 * step) < step
+        tiles = [
+            jnp.where(
+                upper,
+                tiles[i] + pltpu.roll(tiles[i], 8 - step, 0),
+                tiles[i + step] + pltpu.roll(tiles[i + step], step, 0),
+            )
+            for i in range(step)
+        ]
+    return tiles[0]
+
+
+def fold(x):
+    total = x[0:8]
+    for b in range(1, x.shape[0] // 8):
+        total = total + x[8 * b : 8 * b + 8]
+    return total
+
+
+def stencil_stage(proj, curf, shifts, rows_ref, ready):
     sub = iota((8, 128), 0)
     for g in range(4):
         lanes = slice(g * 128, (g + 1) * 128)
@@ -143,13 +171,15 @@
         home = (sub - dr >= 0) & (sub - dr < 8)
         cur = [curf[q, :, lanes] for q in range(RHS)]
 
+        ready(g)
+
         def body(j, carry):
-            tiles = [jnp.zeros((8, 128), F32) for _ in range(RHS)]
+            parts = [[] for _ in range(RHS)]
             for i in range(8):
                 weight = proj[i * 8 + j, :, lanes].astype(F32)
                 for q in range(RHS):
-                    line = jnp.sum(weight * cur[q], axis=0, keepdims=True)
-                    tiles[q] = jnp.where(sub == i, jnp.broadcast_to(line, (8, 128)), tiles[q])
+                    parts[q].append(fold(weight * cur[q]))
+            tiles = [row_sums(part) for part in parts]
             for q in range(RHS):
                 moved = tiles[q]
                 for o in OFFSETS:
@@ -164,7 +194,7 @@
 def spread_stage(rows_ref, shifts, place, left_ref, grid_ref, send_ref):
     sub = iota((64, 128), 0)
     lane = iota((64, 128), 1)
-    own = (sub // 8) == (lane // 16)
+    own = jnp.where((sub // 8) == (lane // 16), 1.0, 0.0).astype(BF16)
     for g in range(4):
         lanes = slice(g * 128, (g + 1) * 128)
         dc = jnp.broadcast_to(shifts[1:2, lanes], (8, 128))
@@ -182,9 +212,9 @@
                 if j in EDGE_SLOT:
                     pieces.append((EDGE_SLOT[j], jnp.where(home, 0.0, moved)))
                 for slot, piece in pieces:
-                    wide = jnp.where(own, jnp.concatenate([piece] * 8, axis=0), 0.0)
+                    pair = jnp.concatenate([piece] * 2, axis=0).astype(BF16)
                     left_ref[pl.ds(pl.multiple_of(idx * 64, 64), 64), slot * 128 : (slot + 1) * 128] = (
-                        wide.astype(BF16)
+                        jnp.concatenate([pair] * 4, axis=0) * own
                     )
             return carry
 
@@ -423,68 +453,229 @@
             ].T * (1.0 / 16777216)
 
 
+def edge_stage(curf, edge_row, edge_col):
+    lane = iota((16, 128), 1)
+    place = lax.rem(lane, 16)
+
+    def body(m, carry):
+        q, at = m // 4, pl.ds(pl.multiple_of(lax.rem(m, 4) * 16, 16), 16)
+        here = pl.ds(pl.multiple_of(m * 16, 16), 16)
+        tiles = [curf[q, at, t * 128 : (t + 1) * 128] for t in range(4)]
+        edge_row[here, :] = jnp.where(lane < 64, tiles[0], tiles[3]).astype(BF16)
+        packed = jnp.zeros((16, 128), F32)
+        for t in range(4):
+            packed = jnp.where(place == t, pltpu.roll(tiles[t], (t - 15) % 128, 1), packed)
+            packed = jnp.where(place == 4 + t, pltpu.roll(tiles[t], 4 + t, 1), packed)
+        edge_col[here, :] = packed.astype(BF16)
+        return carry
+
+    lax.fori_loop(0, 8, body, 0)
+
+
+def partner_stage(curf, partners, edges, picked):
+    lane = iota((16, 128), 1)
+    place = lax.rem(lane, 16)
+
+    def body(m, carry):
+        q, at = m // 4, pl.ds(pl.multiple_of(lax.rem(m, 4) * 16, 16), 16)
+        here = pl.ds(pl.multiple_of(m * 16, 16), 16)
+        near = lambda dr, dc: edges[edge_slot(dr, dc), here, :].astype(F32)
+        middle = [near(-1, 0)]
+        middle += [curf[q, at, t * 128 : (t + 1) * 128] for t in range(4)]
+        middle += [near(1, 0)]
+        left, right = near(0, -1), near(0, 1)
+        from_right = [near(-1, 1), right, right, right, right, near(1, 1)]
+        from_left = [near(-1, -1), left, left, left, left, near(1, -1)]
+        columns = {0: middle, 1: [], -1: []}
+        for e in range(6):
+            inner = e in (1, 2, 3, 4)
+            t = e - 1
+            outside = pltpu.roll(from_right[e], (11 - t) % 128 if inner else 15, 1)
+            columns[1].append(jnp.where(place == 15, outside, pltpu.roll(middle[e], 127, 1)))
+            outside = pltpu.roll(from_left[e], (-t) % 128 if inner else 113, 1)
+            columns[-1].append(jnp.where(place == 0, outside, pltpu.roll(middle[e], 1, 1)))
+        for t in range(4):
+            lanes = slice(t * 128, (t + 1) * 128)
+            views = {}
+            for dc in (-1, 0, 1):
+                x = columns[dc]
+                views[0, dc] = x[t + 1]
+                views[1, dc] = pltpu.roll(jnp.where(lane < 16, x[t + 2], x[t + 1]), 112, 1)
+                views[-1, dc] = pltpu.roll(jnp.where(lane >= 112, x[t], x[t + 1]), 16, 1)
+            for k in range(1, NEIGH):
+                code = jnp.broadcast_to(partners[k : k + 1, lanes], (16, 128))
+                chosen = views[0, 0]
+                for dr in (-1, 0, 1):
+                    for dc in (-1, 0, 1):
+                        if dr or dc:
+                            chosen = jnp.where(code == 3 * (dr + 1) + dc + 1, views[dr, dc], chosen)
+                picked[k - 1, q, at, lanes] = chosen
+        return carry
+
+    lax.fori_loop(0, 8, body, 0)
+
+
+def near_stage(blocks, k, values, near_ref):
+    def body(m, carry):
+        a0 = pl.multiple_of((m // 4) * 8, 8)
+        lanes = pl.ds(pl.multiple_of(lax.rem(m, 4) * 128, 128), 128)
+        sums = [None] * 16
+        for b in range(4):
+            at = slice(16 * b, 16 * b + 16)
+            current = [values[q, at, lanes] for q in range(RHS)]
+            for a in range(8):
+                weight = blocks[k, a0 + a, at, lanes].astype(F32)
+                for q in range(RHS):
+                    part = fold(weight * current[q])
+                    old = sums[q * 8 + a]
+                    sums[q * 8 + a] = part if old is None else old + part
+        for q in range(RHS):
+            tile = row_sums(sums[q * 8 : q * 8 + 8])
+            if k > 0:
+                tile = tile + near_ref[q, pl.ds(a0, 8), lanes]
+            near_ref[q, pl.ds(a0, 8), lanes] = tile
+        return carry
+
+    lax.fori_loop(0, 32, body, 0)
+
+
+AROUND = [(dr, dc) for dr in (-1, 0, 1) for dc in (-1, 0, 1) if dr or dc]
+
+
+def edge_slot(dr, dc):
+    return AROUND.index((dr, dc))
+
+
+def hop_order():
+    hop = lambda d: min(d, 4 - d)
+    offsets = [
+        (x, y, z, core) for x in range(4) for y in range(4) for z in range(4) for core in range(2)
+    ][1:]
+    return sorted(offsets, key=lambda o: -(hop(o[0]) + hop(o[1]) + hop(o[2])))
+
+
 def slots_wait(ref, count, sem):
     part = ref.at[pl.ds(0, count)]
     pltpu.make_async_copy(part, part, sem).wait()
 
 
-def main_kernel(
-    cur, proj, shifts, green, near,
-    place, pick, row_fwd, row_inv, col_fwd, col_inv, small, small_inv, twist_row, twist_col,
-    out_ref,
-    rows_ref, left_ref, grid_ref, send1, recv1, halo1, slab_ref, mix_ref, flat_ref, send2, recv2,
-    half_ref, wide_ref, green_rows, green_turned, send3, recv3, send4, recv4, tall_ref, pick_rows,
-    sample_ref, curf,
-    ssem, rsem, hsem, lsem,
-):
+TABLES = 10
+
+
+def main_kernel(*refs):
+    cur, shifts, partners, proj_hbm, blocks_hbm, green_hbm = refs[:6]
+    tables_hbm = refs[6 : 6 + TABLES]
+    out_ref = refs[6 + TABLES]
+    scratch = refs[7 + TABLES :]
+    tables = scratch[:TABLES]
+    place, pick, row_fwd, row_inv, col_fwd, col_inv, small, small_inv, twist_row, twist_col = tables
+    (
+        proj, blocks, green, rows_ref, left_ref, grid_ref, send1, recv1, halo1, slab_ref, mix_ref,
+        flat_ref, send2, recv2, half_ref, wide_ref, green_rows, green_turned, send3, recv3, send4,
+        recv4, tall_ref, pick_rows, sample_ref, curf, edge_row, edge_col, edges, picked, near_ref,
+        ssem, rsem, hsem, lsem, esem_out, esem_in, psem, nsem, tsem, entered,
+    ) = scratch[TABLES:]
     r, c = lax.axis_index("row"), lax.axis_index("col")
     me = r * 16 + c
+    core, y_low, z = c & 1, lax.shift_right_logical(c, 1) & 1, lax.shift_right_logical(c, 2)
+    x, y = lax.shift_right_logical(r, 1), (r & 1) * 2 + y_low
+
+    proj_copies = [
+        pltpu.make_async_copy(
+            proj_hbm.at[:, :, pl.ds(g * 128, 128)], proj.at[:, :, pl.ds(g * 128, 128)], psem.at[g]
+        )
+        for g in range(4)
+    ]
+    table_copies = [pltpu.make_async_copy(a, b, tsem.at[i]) for i, (a, b) in enumerate(zip(tables_hbm, tables))]
+    green_copy = pltpu.make_async_copy(green_hbm, green, tsem.at[TABLES])
+    block_copies = [pltpu.make_async_copy(blocks_hbm.at[k], blocks.at[k], nsem.at[k]) for k in range(NEIGH)]
+    for copy in proj_copies:
+        copy.start()
+    table_copies[0].start()
+
     barrier = pltpu.get_barrier_semaphore()
 
-    def peer(k):
-        d = lax.rem(me + k, 128)
-        return d, (d // 16, lax.rem(d, 16))
-
-    def greet(k, carry):
-        pl.semaphore_signal(barrier, inc=1, device_id=peer(k)[1], device_id_type=MESH)
-        return carry
-
+    def greet_column(k, carry):
+        pl.semaphore_signal(barrier, inc=1, device_id=(r, (c + k) & 15), device_id_type=MESH)
+        return carry
+
+    def greet_row(k, carry):
+        pl.semaphore_signal(barrier, inc=1, device_id=((r + k) & 7, c), device_id_type=MESH)
+        return carry
+
+    lax.fori_loop(1, 8, greet_row, 0)
+    lax.fori_loop(1, 16, greet_column, 0)
     zero = jnp.zeros((48, 128), BF16)
     recv4[0] = zero
     recv4[17] = zero
-    lax.fori_loop(1, 128, greet, 0)
     curf[...] = cur[...].astype(BF16).astype(F32)
-    stencil_stage(proj, curf, shifts, rows_ref)
+    edge_stage(curf, edge_row, edge_col)
+    stencil_stage(proj, curf, shifts, rows_ref, lambda g: proj_copies[g].wait())
+    for copy in table_copies[1:]:
+        copy.start()
+    green_copy.start()
+    for copy in block_copies:
+        copy.start()
+    pl.semaphore_wait(barrier, 22)
+
+    def tell_column(k, carry):
+        pl.semaphore_signal(entered, inc=1, device_id=(r, (c + k) & 15), device_id_type=MESH)
+        return carry
+
+    lax.fori_loop(1, 16, tell_column, 0)
+    table_copies[0].wait()
     spread_stage(rows_ref, shifts, place, left_ref, grid_ref, send1)
-    pl.semaphore_wait(barrier, 127)
+    pl.semaphore_wait(entered, 15)
+
+    def remote(source, target, send_sem, recv_sem, where):
+        return pltpu.make_async_remote_copy(
+            source, target, send_sem, recv_sem, device_id=where, device_id_type=MESH
+        )
 
     def to_column(send, recv, slot, index):
-        def go(k, carry):
-            d = lax.rem(c + k, 16)
-            pltpu.make_async_remote_copy(
-                send.at[d], recv.at[slot], ssem.at[index], rsem.at[index], device_id=(r, d), device_id_type=MESH
-            ).start()
-            return carry
-
-        lax.fori_loop(1, 16, go, 0)
+        for dx, dy, dz, dcore in hop_order():
+            if dx == 0 and dy < 2:
+                d = ((z + dz) & 3) * 4 + (y_low ^ dy) * 2 + (core ^ dcore)
+                remote(send.at[d], recv.at[slot], ssem.at[index], rsem.at[index], (r, d)).start()
+
+    @pl.when(r > 0)
+    def _():
+        remote(send1.at[16], halo1.at[c], ssem.at[4], hsem.at[0], (r - 1, 15)).start()
+
+    @pl.when(r < 7)
+    def _():
+        remote(send1.at[17], halo1.at[c], ssem.at[5], hsem.at[0], (r + 1, 0)).start()
 
     to_column(send1, recv1, c, 0)
-
-    @pl.when(r > 0)
-    def _():
-        pltpu.make_async_remote_copy(
-            send1.at[16], halo1.at[c], ssem.at[4], hsem.at[0], device_id=(r - 1, 15), device_id_type=MESH
-        ).start()
-
-    @pl.when(r < 7)
-    def _():
-        pltpu.make_async_remote_copy(
-            send1.at[17], halo1.at[c], ssem.at[5], hsem.at[0], device_id=(r + 1, 0), device_id_type=MESH
-        ).start()
-
     own = pltpu.make_async_copy(send1.at[c], recv1.at[c], lsem.at[0])
     own.start()
+
+    def exists(dr, dc):
+        there = None
+        for move, at, last in ((dr, r, 7), (dc, c, 15)):
+            test = at < last if move > 0 else at > 0
+            if move:
+                there = test if there is None else there & test
+        return there
+
+    def edge_copy(dr, dc):
+        target = edge_slot(-dr, -dc)
+        return remote(
+            edge_row if dr else edge_col, edges.at[target], esem_out.at[edge_slot(dr, dc)],
+            esem_in.at[target], (r + dr, c + dc),
+        )
+
+    for dr, dc in AROUND:
+        @pl.when(exists(dr, dc))
+        def _():
+            edge_copy(dr, dc).start()
+
+    green_copy.wait()
     turn_green(green, green_rows, green_turned)
+    block_copies[0].wait()
+    near_stage(blocks, 0, curf, near_ref)
+    for copy in table_copies[1:]:
+        copy.wait()
     own.wait()
     has_halo = ((c == 0) & (r > 0)) | ((c == 15) & (r < 7))
     slots_wait(recv1, 15, rsem.at[0])
@@ -496,32 +687,41 @@
     row_forward_stage(recv1, halo1, has_halo, slab_ref, twist_row, row_fwd, mix_ref, flat_ref, send2)
 
     def to_all(send, recv, index):
-        def go(k, carry):
-            d, where = peer(k)
-            pltpu.make_async_remote_copy(
-                send.at[d], recv.at[me], ssem.at[index], rsem.at[index], device_id=where, device_id_type=MESH
-            ).start()
-            return carry
-
         own = pltpu.make_async_copy(send.at[me], recv.at[me], lsem.at[index])
         own.start()
-        lax.fori_loop(1, 128, go, 0)
-        own.wait()
-        slots_wait(recv, 127, rsem.at[index])
-
-    to_all(send2, recv2, 1)
+        for dx, dy, dz, dcore in hop_order():
+            px, py, pz, pcore = (x + dx) & 3, (y + dy) & 3, (z + dz) & 3, core ^ dcore
+            row = px * 2 + lax.shift_right_logical(py, 1)
+            col = pz * 4 + (py & 1) * 2 + pcore
+            remote(send.at[row * 16 + col], recv.at[me], ssem.at[index], rsem.at[index], (row, col)).start()
+        return own
+
+    own = to_all(send2, recv2, 1)
+    for dr, dc in AROUND:
+        @pl.when(exists(dr, dc))
+        def _():
+            back = edges.at[edge_slot(dr, dc)]
+            pltpu.make_async_copy(back, back, esem_in.at[edge_slot(dr, dc)]).wait()
+
+    partner_stage(curf, partners, edges, picked)
+    for k in (1, 2):
+        block_copies[k].wait()
+        near_stage(blocks, k, picked.at[k - 1], near_ref)
+    own.wait()
+    slots_wait(recv2, 127, rsem.at[1])
     column_stage(
         recv2, flat_ref, half_ref, col_fwd, col_inv, small, small_inv, twist_col, green_turned, wide_ref, send3
     )
-    to_all(send3, recv3, 2)
+    own = to_all(send3, recv3, 2)
+    block_copies[3].wait()
+    near_stage(blocks, 3, picked.at[2], near_ref)
+    own.wait()
+    slots_wait(recv3, 127, rsem.at[2])
     row_inverse_stage(recv3, flat_ref, half_ref, row_inv, twist_row, mix_ref, slab_ref, send4)
-    to_column(send4, recv4, c + 1, 3)
 
     def to_neighbour_row(target, slot, index, sem):
         def go(d, carry):
-            pltpu.make_async_remote_copy(
-                send4.at[d], recv4.at[slot], ssem.at[index], hsem.at[sem], device_id=(target, d), device_id_type=MESH
-            ).start()
+            remote(send4.at[d], recv4.at[slot], ssem.at[index], hsem.at[sem], (target, d)).start()
             return carry
 
         lax.fori_loop(0, 16, go, 0)
@@ -537,6 +737,7 @@
     def _():
         to_neighbour_row(r + 1, 0, 7, 2)
 
+    to_column(send4, recv4, c + 1, 3)
     own = pltpu.make_async_copy(send4.at[c], recv4.at[c + 1], lsem.at[3])
     own.start()
     own.wait()
@@ -551,7 +752,7 @@
         slots_wait(recv4, 1, hsem.at[2])
 
     sample_stage(recv4, pick, shifts, tall_ref, pick_rows, sample_ref)
-    far_stage(proj, sample_ref, near, out_ref)
+    far_stage(proj, sample_ref, near_ref, out_ref)
 
     slots_wait(send1, 15, ssem.at[0])
 
@@ -562,6 +763,11 @@
     @pl.when(r < 7)
     def _():
         slots_wait(send1, 1, ssem.at[5])
+
+    for dr, dc in AROUND:
+        @pl.when(exists(dr, dc))
+        def _():
+            pltpu.make_async_copy(edge_row, edge_row, esem_out.at[edge_slot(dr, dc)]).wait()
 
     slots_wait(send2, 127, ssem.at[1])
     slots_wait(send3, 127, ssem.at[2])
@@ -576,16 +782,21 @@
         slots_wait(send4, 16, ssem.at[7])
 
 
-def main_call(cur, proj, shifts, green, near):
+def shards(currents, projection, near_blocks, partners, shifts, green):
     tables = [jnp.asarray(t) for t in make_tables()]
     vmem = pl.BlockSpec(memory_space=pltpu.VMEM)
+    hbm = pl.BlockSpec(memory_space=pltpu.HBM)
     dma = pltpu.SemaphoreType.DMA
     return pl.pallas_call(
         main_kernel,
         out_shape=jax.ShapeDtypeStruct((RHS, BASIS, ER * EC), F32),
-        in_specs=[vmem] * (5 + len(tables)),
+        in_specs=[vmem] * 3 + [hbm] * (3 + len(tables)),
         out_specs=vmem,
-        scratch_shapes=[
+        scratch_shapes=[pltpu.VMEM(t.shape, t.dtype) for t in tables]
+        + [
+            pltpu.VMEM((64, BASIS, 512), BF16),
+            pltpu.VMEM((NEIGH, BASIS, BASIS, 512), BF16),
+            pltpu.VMEM((32, 4096), F32),
             pltpu.VMEM((RHS, 2, 8, 8, 512), F32),
             pltpu.VMEM((256, 1536), BF16),
             pltpu.VMEM((RHS, 2, 272, 256), F32),
@@ -609,90 +820,26 @@
             pltpu.VMEM((12, 8, 128), F32),
             pltpu.VMEM((RHS, 8, 8, 512), F32),
             pltpu.VMEM((RHS, BASIS, 512), F32),
+            pltpu.VMEM((128, 128), BF16),
+            pltpu.VMEM((128, 128), BF16),
+            pltpu.VMEM((8, 128, 128), BF16),
+            pltpu.VMEM((NEIGH - 1, RHS, BASIS, 512), F32),
+            pltpu.VMEM((RHS, BASIS, 512), F32),
             dma((8,)),
             dma((4,)),
             dma((3,)),
             dma((4,)),
+            dma((8,)),
+            dma((8,)),
+            dma((4,)),
+            dma((NEIGH,)),
+            dma((len(tables) + 1,)),
+            pltpu.SemaphoreType.REGULAR,
         ],
         compiler_params=pltpu.CompilerParams(
-            collective_id=0, has_side_effects=True, vmem_limit_bytes=48 * 2**20
+            collective_id=0, has_side_effects=True, vmem_limit_bytes=52 * 2**20
         ),
-    )(cur, proj, shifts, green, near, *tables)
-
-
-def near_kernel(blocks, picked, out_ref):
-    for g in range(4):
-        lanes = slice(g * 128, (g + 1) * 128)
-
-        def body(step, sums):
-            k, b = step // 4, lax.rem(step, 4)
-            at = pl.ds(pl.multiple_of(b * 16, 16), 16)
-            values = [picked[k, q, at, lanes].astype(F32) for q in range(RHS)]
-            sums = list(sums)
-            for a in range(8):
-                weight = blocks[k, a, at, lanes].astype(F32)
-                for q in range(RHS):
-                    product = weight * values[q]
-                    sums[a * 2 + q] = sums[a * 2 + q] + (product[0:8] + product[8:16])
-            return tuple(sums)
-
-        sums = lax.fori_loop(0, 16, body, tuple(jnp.zeros((8, 128), F32) for _ in range(16)))
-        sub = iota((8, 128), 0)
-        for q in range(RHS):
-            tile = jnp.zeros((8, 128), F32)
-            for a in range(8):
-                line = jnp.sum(sums[a * 2 + q], axis=0, keepdims=True)
-                tile = jnp.where(sub == a, jnp.broadcast_to(line, (8, 128)), tile)
-            out_ref[q, :, lanes] = tile
-
-
-def near_call(blocks, picked):
-    return pl.pallas_call(
-        near_kernel,
-        grid=(8,),
-        out_shape=jax.ShapeDtypeStruct((RHS, BASIS, ER * EC), F32),
-        in_specs=[
-            pl.BlockSpec((NEIGH, 8, BASIS, ER * EC), lambda a: (0, a, 0, 0)),
-            pl.BlockSpec((NEIGH, RHS, BASIS, ER * EC), lambda a: (0, 0, 0, 0)),
-        ],
-        out_specs=pl.BlockSpec((RHS, 8, ER * EC), lambda a: (0, a, 0)),
-        compiler_params=pltpu.CompilerParams(vmem_limit_bytes=24 * 2**20),
-    )(blocks, picked)
-
-
-def extended_2(block, sides, width):
-    for axis, dim in sides:
-        count = lax.axis_size(axis)
-        forward = [(i, i + 1) for i in range(count - 1)]
-        backward = [(target, source) for source, target in forward]
-        low = lax.ppermute(
-            lax.slice_in_dim(block, block.shape[dim] - width, None, axis=dim), axis, forward
-        )
-        high = lax.ppermute(lax.slice_in_dim(block, 0, width, axis=dim), axis, backward)
-        block = jnp.concatenate([low, block, high], axis=dim)
-    return block
-
-
-def shards(currents, projection, near_blocks, partners, shifts, green):
-    elements = ER * EC
-    cur_half = currents.astype(BF16)
-    spread = extended_2(cur_half.reshape(RHS, BASIS, ER, EC), (("row", 2), ("col", 3)), 1)
-    views = []
-    for symbol in range(9):
-        row_start, col_start = symbol // 3, symbol % 3
-        views.append(
-            spread[:, :, row_start : row_start + ER, col_start : col_start + EC].reshape(
-                RHS, BASIS, elements
-            )
-        )
-    picked = []
-    for slot in range(NEIGH):
-        chosen = jnp.zeros((RHS, BASIS, elements), BF16)
-        for symbol in range(9):
-            chosen = jnp.where(partners[slot] == symbol, views[symbol], chosen)
-        picked.append(chosen)
-    near = near_call(near_blocks, jnp.stack(picked))
-    return main_call(currents, projection, shifts, green, near)
+    )(currents, shifts, partners, projection, near_blocks, green, *tables)
 
 
 def solution(mesh):

time: 94.6 us -> 53 us (0.56)
  Pallas kernels: 65.6 us -> 44.9 us
  starting transfers between devices: 13.3 us -> 0 us
  waiting for transfers between devices: 4.14 us -> 0 us
  other arithmetic: 2.86 us -> 0 us
    pallas_call x2 -> x1, Pallas kernels: 65.6 us -> 44.9 us  [shards(): pl.pallas_call(main_kernel, out_shape=jax.ShapeDtypeStruct((RHS, BASIS, E...]
    ppermute x4 -> x0, starting transfers between devices: 13.3 us -> none  [the longest x2 7.85 us: extended_2(): lax.ppermute(lax.slice_in_dim(block, block.shape[dim] - width, None, axis...]
    ppermute x4 -> x0, waiting for transfers between devices: 4.14 us -> none  [the longest x2 3.46 us: extended_2(): lax.ppermute(lax.slice_in_dim(block, 0, width, axis=dim), axis, backward)]
    eq x1 -> x0, other arithmetic: 1.13 us -> none  [shards(): chosen = jnp.where(partners[slot] == symbol, views[symbol], chosen)]
    unnamed x27 -> x17, local copies, waits for them, and re-layouts: 6.54 us -> 7.59 us
    reshape x8 -> x0, local copies, waits for them, and re-layouts: 1.02 us -> none  [shards(): spread[:, :, row_start:row_start + ER, col_start:col_start + EC]]
    convert_element_type x1 -> x0, other arithmetic: 0.97 us -> none  [shards(): cur_half = currents.astype(BF16)]
  transfers between devices with their start and end apart: 4 -> 0, of which waited for: 2 -> 0; matrix products, arithmetic and copies ran while one was open for 2% -> 0% of each run, Pallas kernels for 0% -> 0%
where the time goes in v1:
time: 53 us; the launch traced here: 52.6 us
  Pallas kernels  44.9 us (85%)
  local copies, waits for them, and re-layouts  7.59 us (14%)
    pallas_call x1, Pallas kernels, shards(): pl.pallas_call(main_kernel, out_shape=jax.ShapeDtypeStruct((RHS, BASIS, E...  44.9 us
    unnamed x17, local copies, waits for them, and re-layouts  7.59 us

profile of v1, /device:TPU:1, one launch (start us, length us, event | category | flops | bytes accessed | tf_op | source)
XLA Modules:
  0.0 52.6 jit_solution(12172271502804582800)
XLA Ops:
  0.0 0.0 copy-start
  0.0 0.9 %copy-done = bf16[2,256,256]{2,1,0:T(8,128)(2,1)S(1)} copy-done((bf16[2,256,256]{2,1,0:T(8,128)(2,1)S(1)}, bf16[2,256,256]{2,1,0:T(8,128)(2,1)}, u32[]{:S(2)}) %copy-start) | copy-done | bytes 262168
  1.0 0.0 copy-start.1
  1.0 0.9 %copy-done.1 = f32[2,64,512]{2,1,0:T(8,128)S(1)} copy-done((f32[2,64,512]{2,1,0:T(8,128)S(1)}, f32[2,64,512]{2,1,0:T(8,128)}, u32[]{:S(2)}) %copy-start.1) | copy-done | bytes 262168
  1.9 0.0 copy-start.2
  1.9 0.9 %copy-done.2 = f32[2,256,128]{2,1,0:T(8,128)S(1)} copy-done((f32[2,256,128]{2,1,0:T(8,128)S(1)}, f32[2,256,128]{2,1,0:T(8,128)}, u32[]{:S(2)}) %copy-start.2) | copy-done | bytes 262168
  2.9 0.0 copy-start.3
  2.9 0.9 %copy-done.3 = bf16[2,256,256]{2,1,0:T(8,128)(2,1)S(1)} copy-done((bf16[2,256,256]{2,1,0:T(8,128)(2,1)S(1)}, bf16[2,256,256]{2,1,0:T(8,128)(2,1)}, u32[]{:S(2)}) %copy-start.3) | copy-done | bytes 262168
  3.8 0.0 copy-start.4
  3.8 0.9 %copy-done.4 = bf16[2,256,256]{2,1,0:T(8,128)(2,1)S(1)} copy-done((bf16[2,256,256]{2,1,0:T(8,128)(2,1)S(1)}, bf16[2,256,256]{2,1,0:T(8,128)(2,1)}, u32[]{:S(2)}) %copy-start.4) | copy-done | bytes 262168
  4.8 0.0 copy-start.5
  4.8 0.8 %copy-done.5 = f32[2,32,128]{2,1,0:T(8,128)S(1)} copy-done((f32[2,32,128]{2,1,0:T(8,128)S(1)}, f32[2,32,128]{2,1,0:T(8,128)}, u32[]{:S(2)}) %copy-start.5) | copy-done | bytes 32792
  5.5 0.0 copy-start.6
  5.5 0.7 %copy-done.6 = s32[4,512]{1,0:T(4,128)S(1)} copy-done((s32[4,512]{1,0:T(4,128)S(1)}, s32[4,512]{1,0:T(4,128)}, u32[]{:S(2)}) %copy-start.6) | copy-done | bytes 8216
  6.2 0.0 copy-start.7
  6.2 0.7 %copy-done.7 = s32[2,512]{1,0:T(2,128)S(1)} copy-done((s32[2,512]{1,0:T(2,128)S(1)}, s32[2,512]{1,0:T(2,128)}, u32[]{:S(2)}) %copy-start.7) | copy-done | bytes 4120
  6.9 44.9 %shard_map.154 = f32[2,64,512]{2,1,0:T(8,128)S(1)} custom-call(f32[2,64,512]{2,1,0:T(8,128)S(1)} %copy-done.1, s32[2,512]{1,0:T(2,128)S(1)} %copy-done.7, s32[4,512]{1,0:T(4,128)S(1)} %copy-done.6, bf16[64,64,512]{2,1,0:T(8,128)(2,1)} %refs_3_.1, bf16[4,64,64,512]{3,2,1,0:T(8,128)(2,1)} %refs_4_.1, f32[32,4096]{1,0:T(8,128)} %refs_5_.1, ...), custom_call_target="tpu_custom_call" | custom-call | tf_op jit(solution)/shard_map/pallas_call | solution.py:790
  51.9 0.7 %copy.18 = f32[2,64,512]{2,1,0:T(8,128)} copy(f32[2,64,512]{2,1,0:T(8,128)S(1)} %shard_map.154) | data formatting | bytes 524288
Async XLA Ops:
  0.0 0.9 %copy-start = (bf16[2,256,256]{2,1,0:T(8,128)(2,1)S(1)}, bf16[2,256,256]{2,1,0:T(8,128)(2,1)}, u32[]{:S(2)}) copy-start(bf16[2,256,256]{2,1,0:T(8,128)(2,1)} %constant.20.clone.refs_8_.refs_9_) | copy-start | bytes 786436
  1.0 0.9 %copy-start.1 = (f32[2,64,512]{2,1,0:T(8,128)S(1)}, f32[2,64,512]{2,1,0:T(8,128)}, u32[]{:S(2)}) copy-start(f32[2,64,512]{2,1,0:T(8,128)} %refs_0_.1) | copy-start | bytes 786436
  1.9 0.9 %copy-start.2 = (f32[2,256,128]{2,1,0:T(8,128)S(1)}, f32[2,256,128]{2,1,0:T(8,128)}, u32[]{:S(2)}) copy-start(f32[2,256,128]{2,1,0:T(8,128)} %constant.26.clone.refs_15_) | copy-start | bytes 786436
  2.9 0.9 %copy-start.3 = (bf16[2,256,256]{2,1,0:T(8,128)(2,1)S(1)}, bf16[2,256,256]{2,1,0:T(8,128)(2,1)}, u32[]{:S(2)}) copy-start(bf16[2,256,256]{2,1,0:T(8,128)(2,1)} %constant.24.clone.refs_13_) | copy-start | bytes 786436
  3.8 0.9 %copy-start.4 = (bf16[2,256,256]{2,1,0:T(8,128)(2,1)S(1)}, bf16[2,256,256]{2,1,0:T(8,128)(2,1)}, u32[]{:S(2)}) copy-start(bf16[2,256,256]{2,1,0:T(8,128)(2,1)} %constant.23.clone.refs_12_) | copy-start | bytes 786436
  4.8 0.8 %copy-start.5 = (f32[2,32,128]{2,1,0:T(8,128)S(1)}, f32[2,32,128]{2,1,0:T(8,128)}, u32[]{:S(2)}) copy-start(f32[2,32,128]{2,1,0:T(8,128)} %constant.25.clone.refs_14_) | copy-start | bytes 98308
  5.5 0.7 %copy-start.6 = (s32[4,512]{1,0:T(4,128)S(1)}, s32[4,512]{1,0:T(4,128)}, u32[]{:S(2)}) copy-start(s32[4,512]{1,0:T(4,128)} %refs_2_.1) | copy-start | bytes 24580
  6.2 0.7 %copy-start.7 = (s32[2,512]{1,0:T(2,128)S(1)}, s32[2,512]{1,0:T(2,128)}, u32[]{:S(2)}) copy-start(s32[2,512]{1,0:T(2,128)} %refs_1_.1) | copy-start | bytes 12292

commit v2 on v1

--- a/solution.py
+++ b/solution.py
@@ -563,7 +563,7 @@
 
 
 def main_kernel(*refs):
-    cur, shifts, partners, proj_hbm, blocks_hbm, green_hbm = refs[:6]
+    cur_hbm, shifts_hbm, partners_hbm, proj_hbm, blocks_hbm, green_hbm = refs[:6]
     tables_hbm = refs[6 : 6 + TABLES]
     out_ref = refs[6 + TABLES]
     scratch = refs[7 + TABLES :]
@@ -573,7 +573,7 @@
         proj, blocks, green, rows_ref, left_ref, grid_ref, send1, recv1, halo1, slab_ref, mix_ref,
         flat_ref, send2, recv2, half_ref, wide_ref, green_rows, green_turned, send3, recv3, send4,
         recv4, tall_ref, pick_rows, sample_ref, curf, edge_row, edge_col, edges, picked, near_ref,
-        ssem, rsem, hsem, lsem, esem_out, esem_in, psem, nsem, tsem, entered,
+        cur, shifts, partners, ssem, rsem, hsem, lsem, esem_out, esem_in, psem, nsem, tsem, csem, entered,
     ) = scratch[TABLES:]
     r, c = lax.axis_index("row"), lax.axis_index("col")
     me = r * 16 + c
@@ -589,7 +589,11 @@
     table_copies = [pltpu.make_async_copy(a, b, tsem.at[i]) for i, (a, b) in enumerate(zip(tables_hbm, tables))]
     green_copy = pltpu.make_async_copy(green_hbm, green, tsem.at[TABLES])
     block_copies = [pltpu.make_async_copy(blocks_hbm.at[k], blocks.at[k], nsem.at[k]) for k in range(NEIGH)]
-    for copy in proj_copies:
+    small_copies = [
+        pltpu.make_async_copy(a, b, csem.at[i])
+        for i, (a, b) in enumerate(((cur_hbm, cur), (shifts_hbm, shifts), (partners_hbm, partners)))
+    ]
+    for copy in small_copies + proj_copies:
         copy.start()
     table_copies[0].start()
 
@@ -608,6 +612,8 @@
     zero = jnp.zeros((48, 128), BF16)
     recv4[0] = zero
     recv4[17] = zero
+    for copy in small_copies:
+        copy.wait()
     curf[...] = cur[...].astype(BF16).astype(F32)
     edge_stage(curf, edge_row, edge_col)
     stencil_stage(proj, curf, shifts, rows_ref, lambda g: proj_copies[g].wait())
@@ -789,8 +795,8 @@
     dma = pltpu.SemaphoreType.DMA
     return pl.pallas_call(
         main_kernel,
-        out_shape=jax.ShapeDtypeStruct((RHS, BASIS, ER * EC), F32),
-        in_specs=[vmem] * 3 + [hbm] * (3 + len(tables)),
+        out_shape=pltpu.VMEM((RHS, BASIS, ER * EC), F32),
+        in_specs=[hbm] * (6 + len(tables)),
         out_specs=vmem,
         scratch_shapes=[pltpu.VMEM(t.shape, t.dtype) for t in tables]
         + [
@@ -825,6 +831,9 @@
             pltpu.VMEM((8, 128, 128), BF16),
             pltpu.VMEM((NEIGH - 1, RHS, BASIS, 512), F32),
             pltpu.VMEM((RHS, BASIS, 512), F32),
+            pltpu.VMEM((RHS, BASIS, 512), F32),
+            pltpu.VMEM((2, 512), jnp.int32),
+            pltpu.VMEM((NEIGH, 512), jnp.int32),
             dma((8,)),
             dma((4,)),
             dma((3,)),
@@ -834,10 +843,11 @@
             dma((4,)),
             dma((NEIGH,)),
             dma((len(tables) + 1,)),
+            dma((3,)),
             pltpu.SemaphoreType.REGULAR,
         ],
         compiler_params=pltpu.CompilerParams(
-            collective_id=0, has_side_effects=True, vmem_limit_bytes=52 * 2**20
+            collective_id=0, has_side_effects=True, vmem_limit_bytes=int(60 * 2**20)
         ),
     )(currents, shifts, partners, projection, near_blocks, green, *tables)
 

time: 53 us -> 47 us (0.89)
  local copies, waits for them, and re-layouts: 7.59 us -> 0.71 us
  Pallas kernels: 44.9 us -> 46.2 us
    unnamed x17 -> x1, local copies, waits for them, and re-layouts: 7.59 us -> 0.71 us
    pallas_call x1, Pallas kernels: 44.9 us -> 46.2 us  [shards(): pl.pallas_call(main_kernel, out_shape=pltpu.VMEM((RHS, BASIS, ER * EC), F...]
where the time goes in v2:
time: 47 us; the launch traced here: 46.9 us
  Pallas kernels  46.2 us (98%)
  local copies, waits for them, and re-layouts  0.71 us (2%)
    pallas_call x1, Pallas kernels, shards(): pl.pallas_call(main_kernel, out_shape=pltpu.VMEM((RHS, BASIS, ER * EC), F...  46.2 us

profile of v2, /device:TPU:1, one launch (start us, length us, event | category | flops | bytes accessed | tf_op | source)
XLA Modules:
  0.0 46.9 jit_solution(12599456179349686014)
XLA Ops:
  0.0 46.2 %shard_map.154 = f32[2,64,512]{2,1,0:T(8,128)S(1)} custom-call(f32[2,64,512]{2,1,0:T(8,128)} %refs_0_.1, s32[2,512]{1,0:T(2,128)} %refs_1_.1, s32[4,512]{1,0:T(4,128)} %refs_2_.1, bf16[64,64,512]{2,1,0:T(8,128)(2,1)} %refs_3_.1, bf16[4,64,64,512]{3,2,1,0:T(8,128)(2,1)} %refs_4_.1, f32[32,4096]{1,0:T(8,128)} %refs_5_.1, ...), custom_call_target="tpu_custom_call" | custom-call | tf_op jit(solution)/shard_map/pallas_call | solution.py:796
  46.2 0.7 %copy.18 = f32[2,64,512]{2,1,0:T(8,128)} copy(f32[2,64,512]{2,1,0:T(8,128)S(1)} %shard_map.154) | data formatting | bytes 524288

commit v3 on v2

--- a/solution.py
+++ b/solution.py
@@ -188,7 +188,7 @@
                 rows_ref[q, 1, j, :, lanes] = jnp.where(home, 0.0, moved)
             return carry
 
-        lax.fori_loop(0, 8, body, 0)
+        lax.fori_loop(0, 8, body, 0, unroll=2)
 
 
 def spread_stage(rows_ref, shifts, place, left_ref, grid_ref, send_ref):
@@ -218,7 +218,7 @@
                     )
             return carry
 
-        lax.fori_loop(0, 4, body, 0)
+        lax.fori_loop(0, 4, body, 0, unroll=4)
         product = dot(left_ref[...], place[...])
         for q in range(RHS):
             for kind in range(2):
@@ -334,16 +334,16 @@
         real, imag = wide_ref[0:256, lanes], wide_ref[256:512, lanes]
         turned = jnp.concatenate([real * cos + imag * sin, imag * cos - real * sin], axis=1)
         high, low = split(turned)
-        spec = dot(high, small[0]) + dot(low, small[0]) + dot(high, small[1])
+        spec = dot(high, small[0]) + dot(low, small[0])
         scale = green[:, lanes]
         spec = spec * jnp.concatenate([scale, scale], axis=1)
         high, low = split(spec)
-        back = dot(high, small_inv[0]) + dot(low, small_inv[0]) + dot(high, small_inv[1])
+        back = dot(high, small_inv[0]) + dot(low, small_inv[0])
         real, imag = back[:, 0:128], back[:, 128:256]
         wide_ref[0:256, lanes] = real * cos - imag * sin
         wide_ref[256:512, lanes] = imag * cos + real * sin
     high, low = split(wide_ref[...])
-    out = dot(inv[0], high) + dot(inv[0], low) + dot(inv[1], high)
+    out = dot(inv[0], high) + dot(inv[0], low)
     to_messages(out, flat_ref, out_ref)
 
 
@@ -413,7 +413,7 @@
                 rows_ref[slot] = moved
                 return carry
 
-            lax.fori_loop(0, 12, body, 0)
+            lax.fori_loop(0, 12, body, 0, unroll=4)
             line = lambda j: rows_ref[j] if 0 <= j < 8 else rows_ref[EDGE_SLOT[j % 8]]
             for j in range(8):
                 moved = line(j)
@@ -435,7 +435,7 @@
                     sums[q] = sums[q] + weight * line
             return tuple(sums)
 
-        sums = lax.fori_loop(0, 8, body, tuple(near_ref[q, :, lanes] for q in range(RHS)))
+        sums = lax.fori_loop(0, 8, body, tuple(near_ref[q, :, lanes] for q in range(RHS)), unroll=2)
         for q in range(RHS):
             out_ref[q, :, lanes] = sums[q]
 
@@ -710,17 +710,16 @@
             pltpu.make_async_copy(back, back, esem_in.at[edge_slot(dr, dc)]).wait()
 
     partner_stage(curf, partners, edges, picked)
-    for k in (1, 2):
-        block_copies[k].wait()
-        near_stage(blocks, k, picked.at[k - 1], near_ref)
+    block_copies[1].wait()
+    near_stage(blocks, 1, picked.at[0], near_ref)
     own.wait()
     slots_wait(recv2, 127, rsem.at[1])
     column_stage(
         recv2, flat_ref, half_ref, col_fwd, col_inv, small, small_inv, twist_col, green_turned, wide_ref, send3
     )
     own = to_all(send3, recv3, 2)
-    block_copies[3].wait()
-    near_stage(blocks, 3, picked.at[2], near_ref)
+    block_copies[2].wait()
+    near_stage(blocks, 2, picked.at[1], near_ref)
     own.wait()
     slots_wait(recv3, 127, rsem.at[2])
     row_inverse_stage(recv3, flat_ref, half_ref, row_inv, twist_row, mix_ref, slab_ref, send4)
@@ -746,6 +745,8 @@
     to_column(send4, recv4, c + 1, 3)
     own = pltpu.make_async_copy(send4.at[c], recv4.at[c + 1], lsem.at[3])
     own.start()
+    block_copies[3].wait()
+    near_stage(blocks, 3, picked.at[2], near_ref)
     own.wait()
     slots_wait(recv4, 15, rsem.at[3])
 

time: 47 us -> 45.3 us (0.964)
  Pallas kernels: 46.2 us -> 44.5 us
    pallas_call x1, Pallas kernels: 46.2 us -> 44.5 us  [shards(): pl.pallas_call(main_kernel, out_shape=pltpu.VMEM((RHS, BASIS, ER * EC), F...]
where the time goes in v3:
time: 45.3 us; the launch traced here: 45.2 us
  Pallas kernels  44.5 us (98%)
  local copies, waits for them, and re-layouts  0.71 us (2%)
    pallas_call x1, Pallas kernels, shards(): pl.pallas_call(main_kernel, out_shape=pltpu.VMEM((RHS, BASIS, ER * EC), F...  44.5 us

profile of v3, /device:TPU:1, one launch (start us, length us, event | category | flops | bytes accessed | tf_op | source)
XLA Modules:
  0.0 45.2 jit_solution(15494284255968795880)
XLA Ops:
  0.0 44.5 %shard_map.154 = f32[2,64,512]{2,1,0:T(8,128)S(1)} custom-call(f32[2,64,512]{2,1,0:T(8,128)} %refs_0_.1, s32[2,512]{1,0:T(2,128)} %refs_1_.1, s32[4,512]{1,0:T(4,128)} %refs_2_.1, bf16[64,64,512]{2,1,0:T(8,128)(2,1)} %refs_3_.1, bf16[4,64,64,512]{3,2,1,0:T(8,128)(2,1)} %refs_4_.1, f32[32,4096]{1,0:T(8,128)} %refs_5_.1, ...), custom_call_target="tpu_custom_call" | custom-call | tf_op jit(solution)/shard_map/pallas_call | solution.py:797
  44.5 0.7 %copy.18 = f32[2,64,512]{2,1,0:T(8,128)} copy(f32[2,64,512]{2,1,0:T(8,128)S(1)} %shard_map.154) | data formatting | bytes 524288

commit v4 on v3

--- a/solution.py
+++ b/solution.py
@@ -248,7 +248,7 @@
         send_ref[k] = message(parts)
         return carry
 
-    lax.fori_loop(0, 16, slab, 0)
+    lax.fori_loop(0, 16, slab, 0, unroll=4)
     full = iota((16, 256), 0)
     send_ref[16] = message(
         [jnp.where(full >= 14, grid_ref[q, 1, 0:16, :], 0.0) for q in range(RHS)]
@@ -263,7 +263,7 @@
         slab_ref[c] = recv[c].astype(F32)
         return carry
 
-    lax.fori_loop(0, 16, widen, 0)
+    lax.fori_loop(0, 16, widen, 0, unroll=4)
 
     @pl.when(has_halo)
     def _():
@@ -299,7 +299,7 @@
                 mix_ref[at(k0 * 16), 128:256] = imag * cos - real * sin
         return carry
 
-    lax.fori_loop(0, 2, rows, 0)
+    lax.fori_loop(0, 2, rows, 0, unroll=2)
     high, low = split(mix_ref[...])
     nt = ((1,), (1,))
     out = dot(table[0], high, nt) + dot(table[1], high, nt) + dot(table[0], low, nt)
@@ -367,7 +367,7 @@
             slab_ref[c, at(16), :] = imag
         return carry
 
-    lax.fori_loop(0, 2, rows, 0)
+    lax.fori_loop(0, 2, rows, 0, unroll=2)
     lane = iota((16, 128), 1)
     for c in range(16):
         rim = jnp.zeros((16, 128), F32)
@@ -413,7 +413,7 @@
                 rows_ref[slot] = moved
                 return carry
 
-            lax.fori_loop(0, 12, body, 0, unroll=4)
+            lax.fori_loop(0, 12, body, 0, unroll=12)
             line = lambda j: rows_ref[j] if 0 <= j < 8 else rows_ref[EDGE_SLOT[j % 8]]
             for j in range(8):
                 moved = line(j)
@@ -607,6 +607,22 @@
         pl.semaphore_signal(barrier, inc=1, device_id=((r + k) & 7, c), device_id_type=MESH)
         return carry
 
+    def greet_next(k, carry):
+        pl.semaphore_signal(barrier, inc=1, device_id=(r + 1, k), device_id_type=MESH)
+        return carry
+
+    def greet_last(k, carry):
+        pl.semaphore_signal(barrier, inc=1, device_id=(r - 1, k), device_id_type=MESH)
+        return carry
+
+    @pl.when((c == 15) & (r < 7))
+    def _():
+        lax.fori_loop(0, 16, greet_next, 0)
+
+    @pl.when((c == 0) & (r > 0))
+    def _():
+        lax.fori_loop(0, 16, greet_last, 0)
+
     lax.fori_loop(1, 8, greet_row, 0)
     lax.fori_loop(1, 16, greet_column, 0)
     zero = jnp.zeros((48, 128), BF16)
@@ -615,23 +631,20 @@
     for copy in small_copies:
         copy.wait()
     curf[...] = cur[...].astype(BF16).astype(F32)
-    edge_stage(curf, edge_row, edge_col)
     stencil_stage(proj, curf, shifts, rows_ref, lambda g: proj_copies[g].wait())
     for copy in table_copies[1:]:
         copy.start()
     green_copy.start()
     for copy in block_copies:
         copy.start()
-    pl.semaphore_wait(barrier, 22)
+    table_copies[0].wait()
+    spread_stage(rows_ref, shifts, place, left_ref, grid_ref, send1)
+    pl.semaphore_wait(barrier, 22 + jnp.where(r > 0, 1, 0) + jnp.where(r < 7, 1, 0))
 
     def tell_column(k, carry):
         pl.semaphore_signal(entered, inc=1, device_id=(r, (c + k) & 15), device_id_type=MESH)
         return carry
 
-    lax.fori_loop(1, 16, tell_column, 0)
-    table_copies[0].wait()
-    spread_stage(rows_ref, shifts, place, left_ref, grid_ref, send1)
-    pl.semaphore_wait(entered, 15)
 
     def remote(source, target, send_sem, recv_sem, where):
         return pltpu.make_async_remote_copy(
@@ -655,6 +668,8 @@
     to_column(send1, recv1, c, 0)
     own = pltpu.make_async_copy(send1.at[c], recv1.at[c], lsem.at[0])
     own.start()
+    lax.fori_loop(1, 16, tell_column, 0)
+    edge_stage(curf, edge_row, edge_col)
 
     def exists(dr, dc):
         there = None
@@ -671,13 +686,12 @@
             esem_in.at[target], (r + dr, c + dc),
         )
 
+    pl.semaphore_wait(entered, 15)
     for dr, dc in AROUND:
         @pl.when(exists(dr, dc))
         def _():
             edge_copy(dr, dc).start()
 
-    green_copy.wait()
-    turn_green(green, green_rows, green_turned)
     block_copies[0].wait()
     near_stage(blocks, 0, curf, near_ref)
     for copy in table_copies[1:]:
@@ -703,6 +717,8 @@
         return own
 
     own = to_all(send2, recv2, 1)
+    green_copy.wait()
+    turn_green(green, green_rows, green_turned)
     for dr, dc in AROUND:
         @pl.when(exists(dr, dc))
         def _():

time: 45.3 us -> 42.5 us (0.938)
  Pallas kernels: 44.5 us -> 41.7 us
    pallas_call x1, Pallas kernels: 44.5 us -> 41.7 us  [shards(): pl.pallas_call(main_kernel, out_shape=pltpu.VMEM((RHS, BASIS, ER * EC), F...]
where the time goes in v4:
time: 42.5 us; the launch traced here: 42.4 us
  Pallas kernels  41.7 us (98%)
  local copies, waits for them, and re-layouts  0.71 us (2%)
    pallas_call x1, Pallas kernels, shards(): pl.pallas_call(main_kernel, out_shape=pltpu.VMEM((RHS, BASIS, ER * EC), F...  41.7 us

profile of v4, /device:TPU:1, one launch (start us, length us, event | category | flops | bytes accessed | tf_op | source)
XLA Modules:
  0.0 42.4 jit_solution(4809192574850726645)
XLA Ops:
  0.0 41.7 %shard_map.154 = f32[2,64,512]{2,1,0:T(8,128)S(1)} custom-call(f32[2,64,512]{2,1,0:T(8,128)} %refs_0_.1, s32[2,512]{1,0:T(2,128)} %refs_1_.1, s32[4,512]{1,0:T(4,128)} %refs_2_.1, bf16[64,64,512]{2,1,0:T(8,128)(2,1)} %refs_3_.1, bf16[4,64,64,512]{3,2,1,0:T(8,128)(2,1)} %refs_4_.1, f32[32,4096]{1,0:T(8,128)} %refs_5_.1, ...), custom_call_target="tpu_custom_call" | custom-call | tf_op jit(solution)/shard_map/pallas_call | solution.py:813
  41.7 0.7 %copy.18 = f32[2,64,512]{2,1,0:T(8,128)} copy(f32[2,64,512]{2,1,0:T(8,128)S(1)} %shard_map.154) | data formatting | bytes 524288

commit v5 on v4

--- a/solution.py
+++ b/solution.py
@@ -188,7 +188,7 @@
                 rows_ref[q, 1, j, :, lanes] = jnp.where(home, 0.0, moved)
             return carry
 
-        lax.fori_loop(0, 8, body, 0, unroll=2)
+        lax.fori_loop(0, 8, body, 0, unroll=4)
 
 
 def spread_stage(rows_ref, shifts, place, left_ref, grid_ref, send_ref):
@@ -435,7 +435,7 @@
                     sums[q] = sums[q] + weight * line
             return tuple(sums)
 
-        sums = lax.fori_loop(0, 8, body, tuple(near_ref[q, :, lanes] for q in range(RHS)), unroll=2)
+        sums = lax.fori_loop(0, 8, body, tuple(near_ref[q, :, lanes] for q in range(RHS)), unroll=4)
         for q in range(RHS):
             out_ref[q, :, lanes] = sums[q]
 

time: 42.5 us -> 42.4 us (level)
  no operation moved by 1% of the time
where the time goes in v5:
time: 42.4 us; the launch traced here: 42.3 us
  Pallas kernels  41.6 us (98%)
  local copies, waits for them, and re-layouts  0.71 us (2%)
    pallas_call x1, Pallas kernels, shards(): pl.pallas_call(main_kernel, out_shape=pltpu.VMEM((RHS, BASIS, ER * EC), F...  41.6 us

profile of v5, /device:TPU:1, one launch (start us, length us, event | category | flops | bytes accessed | tf_op | source)
XLA Modules:
  0.0 42.3 jit_solution(10438224927861754790)
XLA Ops:
  0.0 41.6 %shard_map.154 = f32[2,64,512]{2,1,0:T(8,128)S(1)} custom-call(f32[2,64,512]{2,1,0:T(8,128)} %refs_0_.1, s32[2,512]{1,0:T(2,128)} %refs_1_.1, s32[4,512]{1,0:T(4,128)} %refs_2_.1, bf16[64,64,512]{2,1,0:T(8,128)(2,1)} %refs_3_.1, bf16[4,64,64,512]{3,2,1,0:T(8,128)(2,1)} %refs_4_.1, f32[32,4096]{1,0:T(8,128)} %refs_5_.1, ...), custom_call_target="tpu_custom_call" | custom-call | tf_op jit(solution)/shard_map/pallas_call | solution.py:813
  41.6 0.7 %copy.18 = f32[2,64,512]{2,1,0:T(8,128)} copy(f32[2,64,512]{2,1,0:T(8,128)S(1)} %shard_map.154) | data formatting | bytes 524288
